TPU v7x, 32 devices: a whole 2x2x4 slice. The times are simulated.
32 devices in a mesh: groups: 2 (over y), seq: 4 (over x, core), heads: 4 (over z).
Axes of the slice: x: 2, y: 2, z: 4, core: 2. Of those that a mesh axis runs over, the one named last changes fastest.
Arguments:
- prompt_states: bfloat16 [6144, 7168], P(('groups', 'seq'), 'heads'), parts along dimension 0, may hold values from -6 to 6
- new_states: bfloat16 [512, 7168], P(('groups', 'seq'), 'heads'), parts along dimension 0, may hold values from -6 to 6
- prompt_lengths: int32 [8, 16], P('groups'), parts along dimension 0, may hold values from 1 to 128, 768 in all within a row
- routing: int32 [8, 16], P('groups'), parts along dimension 0, may hold values from 0 to 15, each once within a row
- row_request: int32 [512], P(('groups', 'seq')), parts along dimension 0, may hold values from 0 to 15
- queries: bfloat16 [512, 128, 192], P(('groups', 'seq'), 'heads'), parts along dimension 0, may hold values from -68 to 68
- gain_kv: float32 [512], replicated, may hold values from 0.5 to 1.5
- down_kv: bfloat16 [7168, 576], P('heads'), may hold values from -0.0625 to 0.0625
- absorb_k: bfloat16 [128, 128, 512], P('heads'), may hold values from -0.25 to 0.25
- absorb_v: bfloat16 [128, 512, 128], P('heads'), may hold values from -0.25 to 0.25
- out_proj: bfloat16 [16384, 7168], P('heads', 'seq'), may hold values from -0.1875 to 0.1875
Outputs:
- attended: bfloat16 [512, 7168], P(('groups', 'heads'), 'seq'), parts along dimension 0
There are 2 independent parts, one for each index of `groups`. A program takes and returns all parts, laid end to end along the dimension named above; an argument that names none is the same for every part. Nothing has to cross between parts.
Inputs may be any that keep to these rules, and one draw needn't show every extreme that they name: `prompt_lengths`: each row lists the 16 prompt lengths of one prefill index, packed in this order in its 768 rows; each row sums to 768 and reaches 128. `routing`: each row is a permutation of 0 to 15.
All inputs are finite; a program needn't handle non-finite values.
Results may differ from a plain program's by a relative error of at most 0.012.
The roundings to bfloat16 on the way count: a program that leaves them out, or rounds other values in their place, can miss the bound.
Values may be sent and summed in bfloat16 or wider, within the bound.
A program may use at most 128 MiB of HBM per device.

v0:
```python
import math

import jax
import jax.numpy as jnp
from jax import lax
from jax.sharding import PartitionSpec as P

KVL = 512
ROPE = 64
NOPE = 128
MAXLEN = 128


def rotate(part_e, positions):
    half = ROPE // 2
    order = jnp.arange(half, dtype=jnp.float32)
    freq = 10000.0 ** (-2.0 * order / ROPE)
    angle = positions.astype(jnp.float32)[:, None] * freq[None, :]
    cosine = jnp.cos(angle)
    sine = jnp.sin(angle)
    first_half = part_e[:, :half]
    second_half = part_e[:, half:]
    return jnp.concatenate(
        [first_half * cosine - second_half * sine, first_half * sine + second_half * cosine], axis=1
    )


def finish_latent(projected, gain_kv, positions):
    content = projected[:, :KVL]
    inverse = lax.rsqrt(jnp.mean(content * content, axis=1, keepdims=True) + 1e-06)
    content = content * inverse * gain_kv[None, :]
    return jnp.concatenate([content, rotate(projected[:, KVL:], positions)], axis=1).astype(
        jnp.bfloat16
    )


def per_device(
    prompt_states,
    new_states,
    prompt_lengths,
    routing,
    row_request,
    queries,
    gain_kv,
    down_kv,
    absorb_k,
    absorb_v,
    out_proj,
):
    owners = lax.axis_size("seq")
    own_index = lax.axis_index("seq")
    requests = prompt_lengths.shape[1]
    per_peer = requests // owners
    pr_rows = prompt_states.shape[0]
    dec_rows = new_states.shape[0]
    starts_all = jnp.cumsum(prompt_lengths, axis=1) - prompt_lengths
    my_lengths = prompt_lengths[own_index]
    my_starts = starts_all[own_index]
    row_ids = jnp.arange(pr_rows, dtype=jnp.int32)
    row_start = jnp.max(
        jnp.where(my_starts[None, :] <= row_ids[:, None], my_starts[None, :], 0), axis=1
    )
    prompt_pos = row_ids - row_start
    slot_ids = jnp.arange(requests, dtype=jnp.int32)
    source = slot_ids // per_peer
    slot_req = routing[source, own_index * per_peer + slot_ids % per_peer]
    slot_len = prompt_lengths[source, slot_req]
    token_ids = jnp.arange(dec_rows, dtype=jnp.int32)
    same_slot = row_request[:, None] == row_request[None, :]
    earlier = jnp.sum(
        (same_slot & (token_ids[:, None] > token_ids[None, :])).astype(jnp.int32), axis=1
    )
    row_len = slot_len[row_request]
    new_pos = row_len + earlier
    sent_ids = routing[own_index]
    send_len = my_lengths[sent_ids]
    send_first = my_starts[sent_ids]
    rows_all = jnp.concatenate([prompt_states, new_states], axis=0)
    pos_all = jnp.concatenate([prompt_pos, new_pos], axis=0)
    partial_sums = jnp.dot(rows_all, down_kv, preferred_element_type=jnp.float32)
    latent = finish_latent(lax.psum(partial_sums, "heads"), gain_kv, pos_all)
    prompt_lat = latent[:pr_rows]
    new_lat = latent[pr_rows:]
    offsets = jnp.arange(MAXLEN, dtype=jnp.int32)
    source_rows = jnp.clip(send_first[:, None] + offsets[None, :], 0, pr_rows - 1)
    usable = offsets[None, :] < send_len[:, None]
    kv_cache = lax.all_to_all(
        jnp.where(usable[:, :, None], prompt_lat[source_rows], jnp.zeros((), jnp.bfloat16)),
        "seq",
        split_axis=0,
        concat_axis=0,
        tiled=True,
    )
    softmax_scale = 1.0 / math.sqrt(NOPE + ROPE)
    query_latent = jnp.einsum(
        "thn,hnc->thc", queries[:, :, :NOPE], absorb_k, preferred_element_type=jnp.float32
    ).astype(jnp.bfloat16)
    query_full = jnp.concatenate([query_latent, queries[:, :, NOPE:]], axis=2)
    row_cache = kv_cache[row_request]
    cache_pos = jnp.arange(row_cache.shape[1], dtype=jnp.int32)
    score_cache = (
        jnp.einsum("thc,tpc->thp", query_full, row_cache, preferred_element_type=jnp.float32)
        * softmax_scale
    )
    score_new = (
        jnp.einsum("thc,uc->thu", query_full, new_lat, preferred_element_type=jnp.float32)
        * softmax_scale
    )
    ok_cache = (cache_pos[None, :] < row_len[:, None])[:, None, :]
    ok_new = (same_slot & (token_ids[None, :] <= token_ids[:, None]))[:, None, :]
    peak_score = jnp.maximum(
        jnp.max(jnp.where(ok_cache, score_cache, -jnp.inf), axis=2),
        jnp.max(jnp.where(ok_new, score_new, -jnp.inf), axis=2),
    )
    exp_cache = jnp.where(ok_cache, jnp.exp(score_cache - peak_score[:, :, None]), 0.0)
    exp_new = jnp.where(ok_new, jnp.exp(score_new - peak_score[:, :, None]), 0.0)
    denominator = jnp.sum(exp_cache, axis=2) + jnp.sum(exp_new, axis=2)
    weight_cache = (exp_cache / denominator[:, :, None]).astype(jnp.bfloat16)
    weight_new = (exp_new / denominator[:, :, None]).astype(jnp.bfloat16)
    latent_out = jnp.einsum(
        "thp,tpc->thc", weight_cache, row_cache[:, :, :KVL], preferred_element_type=jnp.float32
    )
    latent_out = latent_out + jnp.einsum(
        "thu,uc->thc", weight_new, new_lat[:, :KVL], preferred_element_type=jnp.float32
    )
    latent_out = latent_out.astype(jnp.bfloat16)
    head_out = jnp.einsum(
        "thc,hcv->thv", latent_out, absorb_v, preferred_element_type=jnp.float32
    ).astype(jnp.bfloat16)
    head_out = head_out.reshape(dec_rows, -1)
    projected = jnp.dot(
        lax.all_gather(head_out, "seq", axis=0, tiled=True),
        out_proj,
        preferred_element_type=jnp.float32,
    )
    return lax.psum_scatter(projected, "heads", scatter_dimension=0, tiled=True).astype(
        jnp.bfloat16
    )


def solution(mesh):
    return jax.shard_map(
        per_device,
        mesh=mesh,
        in_specs=(
            P(("groups", "seq"), "heads"),
            P(("groups", "seq"), "heads"),
            P("groups", None),
            P("groups", None),
            P(("groups", "seq")),
            P(("groups", "seq"), "heads", None),
            P(),
            P("heads", None),
            P("heads", None, None),
            P("heads", None, None),
            P("heads", "seq"),
        ),
        out_specs=P(("groups", "heads"), "seq"),
        check_vma=False,
    )
```

profile of v0, /device:TPU:0, one launch (start us, length us, event | category | flops | bytes accessed | tf_op | source)
XLA Modules:
  0.0 267.2 jit_solution(7014830185433869564)
XLA Ops:
  6.5 0.0 copy-start
  6.5 0.0 all-reduce.2.cloned.1.call-start
  6.5 1.6 copy-done
  8.1 5.5 %fusion.2 = f32[832,576]{0,1:T(8,128)} fusion(bf16[1792,576]{0,1:T(8,128)(2,1)S(1)} %copy-done, bf16[64,1792]{1,0:T(8,128)(2,1)} %param.12, bf16[768,1792]{1,0:T(8,128)(2,1)} %param.11), kind=kOutput, calls=%fused_computation.10 | convolution fusion | flops 1723531264 | bytes 6963200 | tf_op jit(solution)/shard_map/dot_general | solution.py:80
  13.6 0.0 all-reduce.2.cloned.1.call-update
  13.7 0.0 copy-start.6
  13.7 0.0 copy-done.3
  13.7 0.7 gather_fusion
  14.4 0.0 copy-done.2
  14.4 0.2 reduce_window_sum.11
  14.6 0.7 gather_fusion.1
  15.3 0.7 gather_fusion.3
  16.0 0.7 gather_fusion.4
  16.7 0.0 copy-done.7
  16.7 0.8 gather_fusion.2
  17.5 0.1 convert_reduce_fusion
  17.6 0.1 select_reduce_fusion.2
  17.7 0.1 iota_compare_fusion.4
  17.8 0.1 fusion.39
  17.9 83.9 %all-reduce.2.cloned.1.call-done = f32[832,576]{0,1:T(8,128)} async-done(((f32[832,576]{0,1:T(8,128)}), f32[832,576]{0,1:T(8,128)}) %all-reduce.2.cloned.1.call-update) | async-done | bytes 1916944 | tf_op jit(solution)/shard_map/psum | solution.py:81
  101.8 1.8 multiply_reduce_fusion
  103.6 1.5 fusion.35
  105.1 0.2 multiply_convert_fusion
  105.3 0.1 pad_maximum_fusion.1
  105.4 0.1 slice.58
  105.4 0.6 copy.72
  106.1 9.3 %gather_fusion.5 = bf16[2048,576]{1,0:T(8,128)(2,1)} fusion(bf16[768,576]{1,0:T(8,128)(2,1)S(1)} %copy.72, s32[2048]{0:T(1024)S(1)} %fusion.39), kind=kCustom, calls=%fused_computation.5 | custom fusion | bytes 4726784 | tf_op jit(solution)/shard_map/gather | solution.py:88
  115.4 4.4 %copy.73 = bf16[16,128,576]{1,2,0:T(8,128)(2,1)} copy(bf16[16,128,576]{2,1,0:T(8,128)(2,1)} %bitcast.48) | data formatting | bytes 4718592 | tf_op jit(solution)/shard_map/gather | solution.py:88
  119.7 3.3 %broadcast_select_fusion = bf16[16,128,576]{1,2,0:T(8,128)(2,1)} fusion(bf16[16,128,576]{1,2,0:T(8,128)(2,1)} %copy.73, pred[16,128]{1,0:T(8,128)(4,1)S(1)} %iota_compare_fusion.4), kind=kLoop, calls=%fused_computation.17 | loop fusion | flops 1179648 | bytes 4720640 | tf_op jit(solution)/shard_map/jit(_where)/select_n | solution.py:88
  123.0 4.6 %all-to-all-start = ((bf16[16,128,576]{1,2,0:T(8,128)(2,1)}), bf16[16,128,576]{1,2,0:T(8,128)(2,1)}, u32[]{:S(2)}, u32[]{:S(2)}) async-start(bf16[16,128,576]{1,2,0:T(8,128)(2,1)} %broadcast_select_fusion), calls=%async_computation | async-start | bytes 4718592 | tf_op jit(solution)/shard_map/all_to_all | solution.py:87
  127.6 0.0 slice-start
  127.6 0.0 all-gather.2.cloned.1.call-start
  127.7 0.2 copy.94
  127.9 0.8 slice-done
  128.7 2.9 %convert_bitcast_fusion = bf16[64,32,512]{2,0,1:T(8,128)(2,1)S(1)} fusion(bf16[32,128,512]{2,1,0:T(8,128)(2,1)} %param.19, bf16[64,32,128]{2,1,0:T(8,128)(2,1)S(1)} %slice-done), kind=kOutput, calls=%fused_computation.20 | convolution fusion | flops 269484032 | bytes 6815744 | tf_op jit(solution)/shard_map/thn,hnc->thc/dot_general | solution.py:95
  131.6 1.9 pad_maximum_fusion
  133.4 0.1 iota_compare_fusion.3
  133.5 0.1 compare_and_fusion
  133.6 2.6 select_reduce_fusion
  136.2 20.0 %all-to-all-done = bf16[16,128,576]{1,2,0:T(8,128)(2,1)} async-done(((bf16[16,128,576]{1,2,0:T(8,128)(2,1)}), bf16[16,128,576]{1,2,0:T(8,128)(2,1)}, u32[]{:S(2)}, u32[]{:S(2)}) %all-to-all-start) | async-done | bytes 2359328 | tf_op jit(solution)/shard_map/all_to_all | solution.py:87
  156.2 7.9 %gather_fusion.6 = bf16[64,128,576]{1,2,0:T(8,128)(2,1)} fusion(bf16[16,128,576]{1,2,0:T(8,128)(2,1)} %all-to-all-done, s32[1024]{0:T(1024)S(1)} %pad_clamp_fusion.1), kind=kCustom, calls=%fused_computation.6 | custom fusion | bytes 18874624 | tf_op jit(solution)/shard_map/gather | solution.py:99
  164.1 7.4 %select_reduce_fusion.1 = (f32[64,32]{1,0:T(8,128)S(1)}, f32[64,32,128]{2,1,0:T(8,128)S(1)}) fusion(pred[64,128]{1,0:T(8,128)(4,1)S(1)} %iota_compare_fusion.3, bf16[64,128,576]{1,2,0:T(8,128)(2,1)} %gather_fusion.6, bf16[64,32,576]{2,0,1:T(8,128)(2,1)} %pad_maximum_fusion), kind=kOutput, calls=%fused_computation.32 | convolution fusion | flops 302774272 | bytes 12861440 | tf_op jit(solution)/shard_map/thc,tpc->thp/dot_general | solution.py:102
  171.6 0.1 copy.76
  171.7 0.1 copy.77
  171.7 1.5 fusion.20
  173.2 0.6 fusion.19
  173.9 0.1 copy.78
  174.0 1.5 divide_convert_fusion
  175.4 0.1 copy.79
  175.5 0.8 copy.87
  176.3 5.4 %fusion = f32[64,32,512]{2,1,0:T(8,128)S(1)} fusion(bf16[64,128,576]{1,2,0:T(8,128)(2,1)} %gather_fusion.6, f32[64,32,128]{2,1,0:T(8,128)S(1)} %get-tuple-element.8, f32[64,32]{1,0:T(8,128)S(1)} %copy.79, f32[64,32]{1,0:T(8,128)S(1)} %copy.77, pred[64,128]{1,0:T(8,128)(4,1)S(1)} %iota_compare_fusion.3), kind=kOutput, calls=%fused_computation.7 | convolution fusion | flops 269484032 | bytes 13656064 | tf_op jit(solution)/shard_map/thp,tpc->thc/dot_general | solution.py:120
  181.7 0.0 copy-start.5
  181.7 0.7 add_convert_fusion
  182.4 1.5 copy-done.5
  183.9 2.7 fusion.16
  186.6 0.9 copy.112
  187.5 0.0 all-gather.2.cloned.1.call-update
  187.5 0.3 reduce-scatter.2.cloned.1.call-start
  187.8 20.5 %all-gather.2.cloned.1.call-done = bf16[256,4096]{1,0:T(8,128)(2,1)} async-done(((bf16[64,4096]{1,0:T(8,128)(2,1)}), bf16[256,4096]{1,0:T(8,128)(2,1)}) %all-gather.2.cloned.1.call-update) | async-done | bytes 2097168 | tf_op jit(solution)/shard_map/all_gather | solution.py:132
  208.2 11.1 %fusion.58 = f32[256,1792]{1,0:T(8,128)} fusion(bf16[256,4096]{1,0:T(8,128)(2,1)} %all-gather.2.cloned.1.call-done, bf16[4096,1792]{1,0:T(8,128)(2,1)} %param.21), kind=kOutput, calls=%fused_computation.107 | convolution fusion | flops 3758096384 | bytes 18612224 | tf_op jit(solution)/shard_map/dot_general | solution.py:131
  219.4 0.0 reduce-scatter.2.cloned.1.call-update
  219.4 39.6 %reduce-scatter.2.cloned.1.call-done = f32[64,1792]{1,0:T(8,128)} async-done(((f32[256,1792]{1,0:T(8,128)}), f32[64,1792]{1,0:T(8,128)}) %reduce-scatter.2.cloned.1.call-update) | async-done | bytes 458768 | tf_op jit(solution)/shard_map/reduce_scatter | solution.py:136
  259.0 1.7 convert_element_type.44
  260.7 0.0 copy-done.1
  (23 shorter events, 0.1 us)
Async XLA Ops:
  6.5 1.6 copy-start
  6.5 7.1 %copy-start.3 = (s32[4,16]{1,0:T(4,128)S(1)}, s32[4,16]{1,0:T(4,128)}, u32[]{:S(2)}) copy-start(s32[4,16]{1,0:T(4,128)} %param.14) | copy-start | bytes 772
  6.5 95.2 %all-reduce.2.cloned.1.call-start = ((), (), s32[]{:S(2)}) async-start(), calls=%async_computation.2 | async-start | bytes 4128768 | tf_op jit(solution)/shard_map/psum | solution.py:81
  13.6 0.8 copy-start.2
  13.6 3.0 %copy-start.7 = (s32[64]{0:T(128)S(1)}, s32[64]{0:T(128)}, u32[]{:S(2)}) copy-start(s32[64]{0:T(128)} %param.15) | copy-start | bytes 772
  13.7 91.4 %copy-start.6 = (f32[512]{0:T(512)S(1)}, f32[512]{0:T(512)}, u32[]{:S(2)}) copy-start(f32[512]{0:T(512)} %param.17) | copy-start | bytes 6148
  101.8 3.3 %copy-start.4 = (f32[832,576]{0,1:T(8,128)S(1)}, f32[832,576]{0,1:T(8,128)}, u32[]{:S(2)}) copy-start(f32[832,576]{0,1:T(8,128)} %all-reduce.2.cloned.1.call-done) | copy-start | bytes 5750788
  123.0 4.7 %slice-start.1 = ((bf16[64,32,192]{2,1,0:T(8,128)(2,1)}), bf16[64,32,64]{2,1,0:T(8,128)(2,1)S(1)}, s32[]{:S(2)}) async-start(bf16[64,32,192]{2,1,0:T(8,128)(2,1)} %param.16), calls=%async_computation.6 | async-start | bytes 1048576 | tf_op jit(solution)/shard_map/slice | solution.py:98
  123.0 33.2 %all-to-all-start = ((bf16[16,128,576]{1,2,0:T(8,128)(2,1)}), bf16[16,128,576]{1,2,0:T(8,128)(2,1)}, u32[]{:S(2)}, u32[]{:S(2)}) async-start(bf16[16,128,576]{1,2,0:T(8,128)(2,1)} %broadcast_select_fusion), calls=%async_computation | async-start | bytes 4718592 | tf_op jit(solution)/shard_map/all_to_all | solution.py:87
  127.6 1.0 slice-start
  127.6 80.6 %all-gather.2.cloned.1.call-start = ((), (), s32[]{:S(2)}) async-start(), calls=%async_computation.3 | async-start | bytes 2621440 | tf_op jit(solution)/shard_map/all_gather | solution.py:132
  181.7 2.2 copy-start.5
  187.5 71.5 %reduce-scatter.2.cloned.1.call-start = ((), (), s32[]{:S(2)}) async-start(), calls=%async_computation.4 | async-start | bytes 2293760 | tf_op jit(solution)/shard_map/reduce_scatter | solution.py:136
  208.2 52.5 %copy-start.1 = (bf16[1792,576]{0,1:T(8,128)(2,1)S(1)}, bf16[1792,576]{0,1:T(8,128)(2,1)}, u32[]{:S(2)}) copy-start(bf16[1792,576]{0,1:T(8,128)(2,1)} %param.18) | copy-start | bytes 6193156
Sparse Core Ops, SparseCore 0:
  13.8 87.9 all-reduce.1
  187.6 20.5 all-gather.1
  219.5 39.3 reduce-scatter.1
where the time goes:
time: 268 us; the launch traced here: 267 us
  waiting for transfers between devices  164 us (61%)
  matrix products  38.4 us (14%)
  local copies, waits for them, and re-layouts  31.8 us (12%)
  other arithmetic  14.8 us (6%)
  between operations  13.4 us (5%)
  starting transfers between devices  4.93 us (2%)
    psum x1, waiting for transfers between devices, per_device(): latent = finish_latent(lax.psum(partial_sums, 'heads'), gain_kv, pos_all)  83.9 us
    reduce_scatter x1, waiting for transfers between devices, per_device(): lax.psum_scatter(projected, 'heads', scatter_dimension=0, tiled=True)  39.6 us
    all_gather x1, waiting for transfers between devices, per_device(): lax.all_gather(head_out, 'seq', axis=0, tiled=True)  20.5 us
    all_to_all x1, waiting for transfers between devices, per_device(): lax.all_to_all(jnp.where(usable[:, :, None], prompt_lat[source_rows], jnp...  20 us
    gather x2, local copies, waits for them, and re-layouts, per_device(): prompt_lat[source_rows]  13.7 us
    dot_general x1, matrix products, per_device(): jnp.dot(lax.all_gather(head_out, 'seq', axis=0, tiled=True), out_proj, pr...  11.1 us
    gather x1, local copies, waits for them, and re-layouts, per_device(): row_cache = kv_cache[row_request]  7.94 us
    dot_general x1, matrix products, per_device(): jnp.einsum('thc,tpc->thp', query_full, row_cache, preferred_element_type=...  7.43 us
  transfers between devices with their start and end apart: 4, of which 4 were waited for; matrix products, arithmetic and copies ran while one was open for 4% of the time, Pallas kernels for 0%

commit v1 on v0

--- a/solution.py
+++ b/solution.py
@@ -1,8 +1,11 @@
+import functools
 import math
 
 import jax
 import jax.numpy as jnp
 from jax import lax
+from jax.experimental import pallas as pl
+from jax.experimental.pallas import tpu as pltpu
 from jax.sharding import PartitionSpec as P
 
 KVL = 512
@@ -11,27 +14,330 @@
 MAXLEN = 128
 
 
-def rotate(part_e, positions):
+MESH = pl.DeviceIdType.MESH
+
+
+def rotation_tables(positions):
     half = ROPE // 2
     order = jnp.arange(half, dtype=jnp.float32)
     freq = 10000.0 ** (-2.0 * order / ROPE)
     angle = positions.astype(jnp.float32)[:, None] * freq[None, :]
     cosine = jnp.cos(angle)
     sine = jnp.sin(angle)
-    first_half = part_e[:, :half]
-    second_half = part_e[:, half:]
-    return jnp.concatenate(
-        [first_half * cosine - second_half * sine, first_half * sine + second_half * cosine], axis=1
-    )
-
-
-def finish_latent(projected, gain_kv, positions):
-    content = projected[:, :KVL]
-    inverse = lax.rsqrt(jnp.mean(content * content, axis=1, keepdims=True) + 1e-06)
-    content = content * inverse * gain_kv[None, :]
-    return jnp.concatenate([content, rotate(projected[:, KVL:], positions)], axis=1).astype(
-        jnp.bfloat16
-    )
+    return (
+        jnp.concatenate([cosine, cosine], axis=1),
+        jnp.concatenate([-sine, sine], axis=1),
+    )
+
+
+def latent_kernel(
+    heads,
+    seq,
+    x_ref,
+    n_ref,
+    w_ref,
+    gain_ref,
+    cos_ref,
+    sin_ref,
+    cache_ref,
+    new_ref,
+    new_part,
+    out_buf,
+    from_left,
+    from_right,
+    rs_send,
+    rs_left,
+    rs_right,
+    ag_send,
+    ag_recv,
+    x_send,
+    x_recv,
+    sib_send,
+    sib_recv,
+):
+    h = lax.axis_index("heads")
+    s = lax.axis_index("seq")
+    sibling = s + 1 - 2 * lax.rem(s, 2)
+    cp = x_ref.shape[0] // heads
+    pn = n_ref.shape[0] // heads
+    others = seq // 2 - 1
+
+    barrier = pltpu.get_barrier_semaphore()
+
+    def greet(where):
+        pl.semaphore_signal(barrier, inc=1, device_id=where, device_id_type=MESH)
+
+    @pl.when(h > 0)
+    def _():
+        greet({"heads": h - 1})
+
+    @pl.when(h < heads - 1)
+    def _():
+        greet({"heads": h + 1})
+
+    greet({"seq": sibling})
+    for j in range(1, others + 1):
+        greet({"seq": lax.rem(s + 2 * j, seq)})
+    pl.semaphore_wait(
+        barrier,
+        1 + others + jnp.where(h > 0, 1, 0) + jnp.where(h < heads - 1, 1, 0),
+    )
+
+    new_part[...] = jnp.dot(n_ref[...], w_ref[...], preferred_element_type=jnp.float32)
+
+    def partial(c):
+        rows = x_ref[pl.ds(pl.multiple_of(c * cp, 16), cp), :]
+        top = jnp.dot(rows, w_ref[...], preferred_element_type=jnp.float32)
+        return jnp.concatenate([top, new_part[pl.ds(pl.multiple_of(c * pn, 16), pn), :]], axis=0)
+
+    def send_right(c):
+        return pltpu.make_async_remote_copy(
+            src_ref=out_buf.at[c],
+            dst_ref=from_left.at[c],
+            send_sem=rs_send.at[c],
+            recv_sem=rs_left.at[c],
+            device_id={"heads": h + 1},
+            device_id_type=MESH,
+        )
+
+    def send_left(c):
+        return pltpu.make_async_remote_copy(
+            src_ref=out_buf.at[c],
+            dst_ref=from_right.at[c],
+            send_sem=rs_send.at[c],
+            recv_sem=rs_right.at[c],
+            device_id={"heads": h - 1},
+            device_id_type=MESH,
+        )
+
+    for i in range(heads - 1):
+        right, left = heads - 1 - i, i
+
+        @pl.when(h < right)
+        def _():
+            @pl.when(h == 0)
+            def _():
+                out_buf[right] = partial(right).astype(jnp.bfloat16)
+
+            @pl.when(h > 0)
+            def _():
+                mine = partial(right)
+                send_right(right).wait_recv()
+                out_buf[right] = (mine + from_left[right].astype(jnp.float32)).astype(jnp.bfloat16)
+
+            send_right(right).start()
+
+        @pl.when(h > left)
+        def _():
+            @pl.when(h == heads - 1)
+            def _():
+                out_buf[left] = partial(left).astype(jnp.bfloat16)
+
+            @pl.when(h < heads - 1)
+            def _():
+                mine = partial(left)
+                send_left(left).wait_recv()
+                out_buf[left] = (mine + from_right[left].astype(jnp.float32)).astype(jnp.bfloat16)
+
+            send_left(left).start()
+
+    def finish(total):
+        content = total[:, :KVL]
+        inverse = lax.rsqrt(jnp.mean(content * content, axis=1, keepdims=True) + 1e-06)
+        content = (content * inverse * gain_ref[...]).astype(jnp.bfloat16)
+        e = total[:, KVL:]
+        half = ROPE // 2
+        swapped = jnp.concatenate([e[:, half:], e[:, :half]], axis=1)
+        turned = (e * cos_ref[...] + swapped * sin_ref[...]).astype(jnp.bfloat16)
+        mine = pl.ds(pl.multiple_of(h * cp, 16), cp)
+        fresh = pl.ds(pl.multiple_of(h * pn, 16), pn)
+        cache_ref[s, mine, :KVL] = content[:cp]
+        cache_ref[s, mine, KVL:] = turned[:cp]
+        new_ref[fresh, :KVL] = content[cp:]
+        new_ref[fresh, KVL:] = turned[cp:]
+
+    own = partial(h)
+
+    @pl.when(h == 0)
+    def _():
+        send_left(h).wait_recv()
+        finish(own + from_right[h].astype(jnp.float32))
+
+    @pl.when(h == heads - 1)
+    def _():
+        send_right(h).wait_recv()
+        finish(own + from_left[h].astype(jnp.float32))
+
+    @pl.when((h > 0) & (h < heads - 1))
+    def _():
+        send_right(h).wait_recv()
+        send_left(h).wait_recv()
+        finish(own + from_left[h].astype(jnp.float32) + from_right[h].astype(jnp.float32))
+
+    def block(source, c):
+        return cache_ref.at[source, pl.ds(pl.multiple_of(c * cp, 16), cp), :]
+
+    def gather_copies(c, side, where):
+        fresh = new_ref.at[pl.ds(pl.multiple_of(c * pn, 16), pn), :]
+        return [
+            pltpu.make_async_remote_copy(
+                src_ref=ref,
+                dst_ref=ref,
+                send_sem=ag_send.at[side, kind, c],
+                recv_sem=ag_recv.at[kind, c],
+                device_id=where,
+                device_id_type=MESH,
+            )
+            for kind, ref in enumerate((block(s, c), fresh))
+        ]
+
+    def to_right(c):
+        return gather_copies(c, 0, {"heads": h + 1})
+
+    def to_left(c):
+        return gather_copies(c, 1, {"heads": h - 1})
+
+    def over(j, source, c):
+        return pltpu.make_async_remote_copy(
+            src_ref=block(source, c),
+            dst_ref=block(source, c),
+            send_sem=x_send.at[j - 1, c],
+            recv_sem=x_recv.at[j - 1, c],
+            device_id={"seq": lax.rem(s + 2 * j, seq)},
+            device_id_type=MESH,
+        )
+
+    def across(source, c):
+        return pltpu.make_async_remote_copy(
+            src_ref=block(source, c),
+            dst_ref=block(source, c),
+            send_sem=sib_send.at[lax.div(source, 2), c],
+            recv_sem=sib_recv.at[lax.div(source, 2), c],
+            device_id={"seq": sibling},
+            device_id_type=MESH,
+        )
+
+    def spread(c):
+        for j in range(1, others + 1):
+            over(j, s, c).start()
+        across(s, c).start()
+
+    @pl.when(h < heads - 1)
+    def _():
+        for copy in to_right(h):
+            copy.start()
+
+    @pl.when(h > 0)
+    def _():
+        for copy in to_left(h):
+            copy.start()
+
+    spread(h)
+    for k in range(1, heads):
+
+        @pl.when(h - k >= 0)
+        def _():
+            for copy in to_right(h - k):
+                copy.wait_recv()
+
+            @pl.when(h < heads - 1)
+            def _():
+                for copy in to_right(h - k):
+                    copy.start()
+
+            spread(h - k)
+
+        @pl.when(h + k < heads)
+        def _():
+            for copy in to_left(h + k):
+                copy.wait_recv()
+
+            @pl.when(h > 0)
+            def _():
+                for copy in to_left(h + k):
+                    copy.start()
+
+            spread(h + k)
+
+    def relay(c):
+        for j in range(1, others + 1):
+            source = lax.rem(s - 2 * j + seq, seq)
+            over(j, source, c).wait_recv()
+            across(source, c).start()
+
+    relay(h)
+    for k in range(1, heads):
+
+        @pl.when(h - k >= 0)
+        def _():
+            relay(h - k)
+
+        @pl.when(h + k < heads)
+        def _():
+            relay(h + k)
+
+    for c in range(heads):
+        for j in range(others + 1):
+            across(lax.rem(sibling + 2 * j, seq), c).wait_recv()
+
+    for c in range(heads):
+
+        @pl.when(h != c)
+        def _():
+            send_right(c).wait_send()
+
+        @pl.when((c <= h) & (h < heads - 1))
+        def _():
+            for copy in to_right(c):
+                copy.wait_send()
+
+        @pl.when((c >= h) & (h > 0))
+        def _():
+            for copy in to_left(c):
+                copy.wait_send()
+
+        for j in range(others + 1):
+            across(lax.rem(s + 2 * j, seq), c).wait_send()
+        for j in range(1, others + 1):
+            over(j, s, c).wait_send()
+
+
+def latent_rows(prompt_states, new_states, down_kv, gain_kv, cosine, sine):
+    heads = lax.axis_size("heads")
+    seq = lax.axis_size("seq")
+    rows, fresh = prompt_states.shape[0], new_states.shape[0]
+    width = down_kv.shape[1]
+    chunk = rows // heads + fresh // heads
+    others = max(seq // 2 - 1, 1)
+    vmem = pl.BlockSpec(memory_space=pltpu.VMEM)
+    dma = pltpu.SemaphoreType.DMA
+    return pl.pallas_call(
+        functools.partial(latent_kernel, heads, seq),
+        out_shape=(
+            jax.ShapeDtypeStruct((seq, rows, width), jnp.bfloat16),
+            jax.ShapeDtypeStruct((fresh, width), jnp.bfloat16),
+        ),
+        in_specs=[vmem] * 6,
+        out_specs=(vmem, vmem),
+        scratch_shapes=[
+            pltpu.VMEM((fresh, width), jnp.float32),
+            pltpu.VMEM((heads, chunk, width), jnp.bfloat16),
+            pltpu.VMEM((heads, chunk, width), jnp.bfloat16),
+            pltpu.VMEM((heads, chunk, width), jnp.bfloat16),
+            dma((heads,)),
+            dma((heads,)),
+            dma((heads,)),
+            dma((2, 2, heads)),
+            dma((2, heads)),
+            dma((others, heads)),
+            dma((others, heads)),
+            dma((seq // 2, heads)),
+            dma((seq // 2, heads)),
+        ],
+        compiler_params=pltpu.CompilerParams(
+            collective_id=0, has_side_effects=True, vmem_limit_bytes=48 * 1024 * 1024
+        ),
+    )(prompt_states, new_states, down_kv, gain_kv[None, :], cosine, sine)
 
 
 def per_device(
@@ -72,31 +378,34 @@
     )
     row_len = slot_len[row_request]
     new_pos = row_len + earlier
-    sent_ids = routing[own_index]
-    send_len = my_lengths[sent_ids]
-    send_first = my_starts[sent_ids]
-    rows_all = jnp.concatenate([prompt_states, new_states], axis=0)
-    pos_all = jnp.concatenate([prompt_pos, new_pos], axis=0)
-    partial_sums = jnp.dot(rows_all, down_kv, preferred_element_type=jnp.float32)
-    latent = finish_latent(lax.psum(partial_sums, "heads"), gain_kv, pos_all)
-    prompt_lat = latent[:pr_rows]
-    new_lat = latent[pr_rows:]
+    heads = lax.axis_size("heads")
+    head_index = lax.axis_index("heads")
+    cp = pr_rows // heads
+    pn = 16 * -(-dec_rows // (16 * heads))
+    padded = pn * heads - dec_rows
+    my_pos = jnp.concatenate(
+        [
+            lax.dynamic_slice_in_dim(prompt_pos, head_index * cp, cp),
+            lax.dynamic_slice_in_dim(jnp.pad(new_pos, (0, padded)), head_index * pn, pn),
+        ]
+    )
+    cosine, sine = rotation_tables(my_pos)
+    prompt_lat, new_lat = latent_rows(
+        prompt_states, jnp.pad(new_states, ((0, padded), (0, 0))), down_kv, gain_kv, cosine, sine
+    )
+    new_lat = new_lat[:dec_rows]
+    prompt_lat = prompt_lat.reshape(owners * pr_rows, -1)
+    slot_first = source * pr_rows + starts_all[source, slot_req]
     offsets = jnp.arange(MAXLEN, dtype=jnp.int32)
-    source_rows = jnp.clip(send_first[:, None] + offsets[None, :], 0, pr_rows - 1)
-    usable = offsets[None, :] < send_len[:, None]
-    kv_cache = lax.all_to_all(
-        jnp.where(usable[:, :, None], prompt_lat[source_rows], jnp.zeros((), jnp.bfloat16)),
-        "seq",
-        split_axis=0,
-        concat_axis=0,
-        tiled=True,
-    )
     softmax_scale = 1.0 / math.sqrt(NOPE + ROPE)
     query_latent = jnp.einsum(
         "thn,hnc->thc", queries[:, :, :NOPE], absorb_k, preferred_element_type=jnp.float32
     ).astype(jnp.bfloat16)
     query_full = jnp.concatenate([query_latent, queries[:, :, NOPE:]], axis=2)
-    row_cache = kv_cache[row_request]
+    row_first = slot_first[row_request]
+    row_cache = prompt_lat[
+        jnp.clip(row_first[:, None] + offsets[None, :], 0, owners * pr_rows - 1)
+    ]
     cache_pos = jnp.arange(row_cache.shape[1], dtype=jnp.int32)
     score_cache = (
         jnp.einsum("thc,tpc->thp", query_full, row_cache, preferred_element_type=jnp.float32)
@@ -133,8 +442,8 @@
         out_proj,
         preferred_element_type=jnp.float32,
     )
-    return lax.psum_scatter(projected, "heads", scatter_dimension=0, tiled=True).astype(
-        jnp.bfloat16
+    return lax.psum_scatter(
+        projected.astype(jnp.bfloat16), "heads", scatter_dimension=0, tiled=True
     )
 
 

time: 268 us -> 213 us (0.79)
  waiting for transfers between devices: 164 us -> 46.6 us
  Pallas kernels: 0 us -> 59.7 us
  local copies, waits for them, and re-layouts: 31.8 us -> 51.5 us
  matrix products: 38.4 us -> 31.8 us
  other arithmetic: 14.8 us -> 8.83 us
  starting transfers between devices: 4.93 us -> 0.26 us
    psum x1 -> x0, waiting for transfers between devices: 83.9 us -> none  [per_device(): latent = finish_latent(lax.psum(partial_sums, 'heads'), gain_kv, pos_all)]
    pallas_call x0 -> x1, Pallas kernels: none -> 59.7 us  [latent_rows(): pl.pallas_call(functools.partial(latent_kernel, heads, seq), out_shape=(j...]
    all_to_all x1 -> x0, waiting for transfers between devices: 20 us -> none  [per_device(): lax.all_to_all(jnp.where(usable[:, :, None], prompt_lat[source_rows], jnp...]
    gather x5 -> x3, local copies, waits for them, and re-layouts: 22.9 us -> 39.1 us  [the longest x1 37.6 us: per_device(): prompt_lat[jnp.clip(row_first[:, None] + offsets[None, :], 0, owners * pr...]
    reduce_scatter x1, waiting for transfers between devices: 39.6 us -> 25.3 us  [per_device(): lax.psum_scatter(projected.astype(jnp.bfloat16), 'heads', scatter_dimensi...]
    dot_general x1 -> x0, matrix products: 5.52 us -> none  [per_device(): jnp.dot(rows_all, down_kv, preferred_element_type=jnp.float32)]
    all_to_all x1 -> x0, starting transfers between devices: 4.62 us -> none  [per_device(): lax.all_to_all(jnp.where(usable[:, :, None], prompt_lat[source_rows], jnp...]
    unnamed x17 -> x14, local copies, waits for them, and re-layouts: 3.29 us -> 7.43 us
  transfers between devices with their start and end apart: 4 -> 2, of which waited for: 4 -> 2; matrix products, arithmetic and copies ran while one was open for 4% -> 0% of each run, Pallas kernels for 0% -> 0%
where the time goes in v1:
time: 213 us; the launch traced here: 212 us
  Pallas kernels  59.7 us (28%)
  local copies, waits for them, and re-layouts  51.5 us (24%)
  waiting for transfers between devices  46.6 us (22%)
  matrix products  31.8 us (15%)
  between operations  13.6 us (6%)
  other arithmetic  8.83 us (4%)
    pallas_call x1, Pallas kernels, latent_rows(): pl.pallas_call(functools.partial(latent_kernel, heads, seq), out_shape=(j...  59.7 us
    gather x1, local copies, waits for them, and re-layouts, per_device(): prompt_lat[jnp.clip(row_first[:, None] + offsets[None, :], 0, owners * pr...  37.6 us
    reduce_scatter x1, waiting for transfers between devices, per_device(): lax.psum_scatter(projected.astype(jnp.bfloat16), 'heads', scatter_dimensi...  25.3 us
    all_gather x1, waiting for transfers between devices, per_device(): lax.all_gather(head_out, 'seq', axis=0, tiled=True)  21.3 us
    dot_general x1, matrix products, per_device(): jnp.dot(lax.all_gather(head_out, 'seq', axis=0, tiled=True), out_proj, pr...  10.7 us
    unnamed x14, local copies, waits for them, and re-layouts  7.43 us
    dot_general x1, matrix products, per_device(): jnp.einsum('thc,tpc->thp', query_full, row_cache, preferred_element_type=...  7 us
  transfers between devices with their start and end apart: 2, of which 2 were waited for; matrix products, arithmetic and copies ran while one was open for 0% of the time, Pallas kernels for 0%

profile of v1, /device:TPU:0, one launch (start us, length us, event | category | flops | bytes accessed | tf_op | source)
XLA Modules:
  0.0 212.3 jit_solution(2499363843474029171)
XLA Ops:
  6.5 0.0 copy-start
  6.5 0.0 all-gather.2.cloned.1.call-start
  6.5 0.7 compare_select_fusion.1
  7.2 0.8 convert_reduce_fusion
  8.0 0.0 slice-start.1
  8.1 0.8 compare_and_fusion
  8.9 0.9 reduce_window_sum.11
  9.7 0.7 sub.31
  10.4 0.0 copy-done
  10.4 0.7 gather_fusion
  11.2 0.0 copy-start.2
  11.2 0.0 copy-start.3
  11.2 1.4 gather_fusion.1
  12.6 0.7 gather_fusion.3
  13.3 0.1 select_reduce_fusion.2
  13.4 0.8 gather_fusion.2
  14.2 0.1 iota_compare_fusion.3
  14.3 3.1 %copy.63.w_ref = bf16[1792,576]{1,0:T(8,128)(2,1)S(1)} copy(bf16[1792,576]{0,1:T(8,128)(2,1)} %param.18) | data formatting | bytes 4128768 | tf_op args[7]
  17.4 0.8 gather_fusion.4
  18.2 0.1 fusion.27
  18.3 0.0 slice-done.1
  18.3 1.0 copy.79
  19.3 0.1 dynamic_slice.10
  19.4 0.1 dynamic_slice.11
  19.5 0.1 add_convert_fusion.1
  19.5 0.5 fusion.25
  20.0 0.1 pad_maximum_fusion.1
  20.1 0.0 copy-done.2
  20.1 0.0 copy-done.3
  20.2 0.0 copy-start.1
  20.2 1.8 copy-done.1
  21.9 59.7 %shard_map.109 = (bf16[4,768,576]{2,1,0:T(8,128)(2,1)}, bf16[64,576]{1,0:T(8,128)(2,1)S(1)}) custom-call(bf16[768,1792]{1,0:T(8,128)(2,1)S(1)} %copy-done.1, bf16[64,1792]{1,0:T(8,128)(2,1)S(1)} %copy-done.2, bf16[1792,576]{1,0:T(8,128)(2,1)S(1)} %copy.63.w_ref, f32[1,512]{1,0:T(1,128)S(1)} %bitcast.39, f32[208,64]{1,0:T(8,128)S(1)} %get-tuple-element.16.cos_ref, ...), custom_call_target="tpu_custom_call" | custom-call | tf_op jit(solution)/shard_map/pallas_call | solution.py:314
  81.6 0.0 slice-start
  81.6 37.6 %gather_fusion.5 = bf16[8192,576]{1,0:T(8,128)(2,1)} fusion(bf16[3072,576]{1,0:T(8,128)(2,1)} %bitcast.40, s32[8192]{0:T(1024)S(1)} %fusion.27), kind=kCustom, calls=%fused_computation.5 | custom fusion | bytes 18907136 | tf_op jit(solution)/shard_map/gather | solution.py:406
  119.3 0.0 slice-done
  119.3 0.0 copy-start.5
  119.3 3.0 %convert_bitcast_fusion = bf16[64,32,512]{2,0,1:T(8,128)(2,1)S(1)} fusion(bf16[32,128,512]{2,1,0:T(8,128)(2,1)} %param.19, bf16[64,32,128]{2,1,0:T(8,128)(2,1)S(1)} %slice-done), kind=kOutput, calls=%fused_computation.15 | convolution fusion | flops 269484032 | bytes 6815744 | tf_op jit(solution)/shard_map/thn,hnc->thc/dot_general | solution.py:401
  122.2 0.0 copy-done.5
  122.2 0.4 pad_maximum_fusion
  122.6 7.0 %select_reduce_fusion.1 = (f32[64,32]{1,0:T(8,128)S(1)}, f32[64,32,128]{2,1,0:T(8,128)S(1)}) fusion(pred[64,128]{1,0:T(8,128)(4,1)S(1)} %iota_compare_fusion.3, bf16[64,128,576]{2,1,0:T(8,128)(2,1)} %bitcast.41, bf16[64,32,576]{2,0,1:T(8,128)(2,1)S(1)} %pad_maximum_fusion), kind=kOutput, calls=%fused_computation.25 | convolution fusion | flops 302774272 | bytes 12861440 | tf_op jit(solution)/shard_map/thc,tpc->thp/dot_general | solution.py:411
  129.6 0.1 copy.66
  129.7 3.6 %select_reduce_fusion = (f32[64,32]{0,1:T(8,128)S(1)}, f32[64,32,64]{0,2,1:T(8,128)}) fusion(pred[64,64]{0,1:T(8,128)(4,1)S(1)} %compare_and_fusion, bf16[64,576]{1,0:T(8,128)(2,1)S(1)} %get-tuple-element.8, bf16[64,32,64]{2,0,1:T(8,128)(2,1)} %copy.79, bf16[64,32,512]{2,0,1:T(8,128)(2,1)S(1)} %convert_bitcast_fusion), kind=kOutput, calls=%fused_computation.24 | convolution fusion | flops 156104704 | bytes 2969600 | tf_op jit(solution)/shard_map/thc,uc->thu/dot_general | solution.py:415
  133.4 0.1 copy.67
  133.5 1.5 fusion.16
  134.9 0.7 fusion.15
  135.6 0.1 copy.68
  135.7 1.5 divide_convert_fusion
  137.2 0.1 copy.69
  137.2 0.8 copy.75
  138.0 4.3 %fusion = f32[64,32,512]{2,1,0:T(8,128)S(1)} fusion(bf16[64,128,576]{2,1,0:T(8,128)(2,1)} %bitcast.42, f32[64,32,128]{2,1,0:T(8,128)S(1)} %get-tuple-element.13, f32[64,32]{1,0:T(8,128)S(1)} %copy.69, f32[64,32]{1,0:T(8,128)S(1)} %copy.67, pred[64,128]{1,0:T(8,128)(4,1)S(1)} %iota_compare_fusion.3), kind=kOutput, calls=%fused_computation.6 | convolution fusion | flops 269484032 | bytes 13656064 | tf_op jit(solution)/shard_map/thp,tpc->thc/dot_general | solution.py:429
  142.3 0.0 copy-start.4
  142.3 0.7 add_convert_fusion
  143.0 1.5 copy-done.4
  144.5 2.5 %fusion.12 = bf16[32,8,8,128]{3,2,1,0:T(8,128)(2,1)S(1)} fusion(bf16[32,512,128]{2,1,0:T(8,128)(2,1)S(1)} %copy-done.4, bf16[64,32,512]{2,1,0:T(8,128)(2,1)S(1)} %add_convert_fusion), kind=kOutput, calls=%fused_computation.19 | convolution fusion | flops 268697600 | bytes 6815744 | tf_op jit(solution)/shard_map/thc,hcv->thv/dot_general | solution.py:436
  147.0 0.9 copy.96
  147.9 0.0 all-gather.2.cloned.1.call-update
  147.9 0.3 reduce-scatter.2.cloned.1.call-start
  148.2 21.3 %all-gather.2.cloned.1.call-done = bf16[256,4096]{1,0:T(8,128)(2,1)} async-done(((bf16[64,4096]{1,0:T(8,128)(2,1)}), bf16[256,4096]{1,0:T(8,128)(2,1)}) %all-gather.2.cloned.1.call-update) | async-done | bytes 2097168 | tf_op jit(solution)/shard_map/all_gather | solution.py:441
  169.5 10.7 %convolution_convert_fusion = bf16[256,1792]{1,0:T(8,128)(2,1)} fusion(bf16[256,4096]{1,0:T(8,128)(2,1)} %all-gather.2.cloned.1.call-done, bf16[4096,1792]{1,0:T(8,128)(2,1)} %param.21), kind=kOutput, calls=%fused_computation.12 | convolution fusion | flops 3758555136 | bytes 17694720 | tf_op jit(solution)/shard_map/dot_general | solution.py:440
  180.2 0.0 reduce-scatter.2.cloned.1.call-update
  180.2 25.3 %reduce-scatter.2.cloned.1.call-done = bf16[64,1792]{1,0:T(8,128)(2,1)} async-done(((bf16[256,1792]{1,0:T(8,128)(2,1)}), bf16[64,1792]{1,0:T(8,128)(2,1)}) %reduce-scatter.2.cloned.1.call-update) | async-done | bytes 229392 | tf_op jit(solution)/shard_map/reduce_scatter | solution.py:445
  (10 shorter events, 0.1 us)
Async XLA Ops:
  6.5 3.9 %copy-start = (s32[4,16]{1,0:T(4,128)S(1)}, s32[4,16]{1,0:T(4,128)}, u32[]{:S(2)}) copy-start(s32[4,16]{1,0:T(4,128)} %param.14) | copy-start | bytes 772
  6.5 162.9 %all-gather.2.cloned.1.call-start = ((), (), s32[]{:S(2)}) async-start(), calls=%async_computation.1 | async-start | bytes 2621440 | tf_op jit(solution)/shard_map/all_gather | solution.py:441
  8.0 10.3 %slice-start.1 = ((bf16[64,32,192]{2,1,0:T(8,128)(2,1)}), bf16[64,32,64]{2,1,0:T(8,128)(2,1)S(1)}, s32[]{:S(2)}) async-start(bf16[64,32,192]{2,1,0:T(8,128)(2,1)} %param.16), calls=%async_computation.4 | async-start | bytes 1048576 | tf_op jit(solution)/shard_map/slice | solution.py:404
  11.2 9.0 %copy-start.2 = (bf16[64,1792]{1,0:T(8,128)(2,1)S(1)}, bf16[64,1792]{1,0:T(8,128)(2,1)}, u32[]{:S(2)}) copy-start(bf16[64,1792]{1,0:T(8,128)(2,1)} %n_ref.1) | copy-start | bytes 688132
  11.2 9.0 %copy-start.3 = (f32[512]{0:T(512)S(1)}, f32[512]{0:T(512)}, u32[]{:S(2)}) copy-start(f32[512]{0:T(512)} %param.17) | copy-start | bytes 6148
  20.2 1.8 copy-start.1
  81.6 37.6 %slice-start = ((bf16[64,32,192]{2,1,0:T(8,128)(2,1)}), bf16[64,32,128]{2,1,0:T(8,128)(2,1)S(1)}, s32[]{:S(2)}) async-start(bf16[64,32,192]{2,1,0:T(8,128)(2,1)} %param.16), calls=%async_computation.3 | async-start | bytes 1048576 | tf_op jit(solution)/shard_map/slice | solution.py:402
  119.3 3.0 %copy-start.5 = (bf16[64,32,64]{2,0,1:T(8,128)(2,1)S(1)}, bf16[64,32,64]{2,0,1:T(8,128)(2,1)}, u32[]{:S(2)}) copy-start(bf16[64,32,64]{2,0,1:T(8,128)(2,1)} %copy.79) | copy-start | bytes 786436
  142.3 2.2 %copy-start.4 = (bf16[32,512,128]{2,1,0:T(8,128)(2,1)S(1)}, bf16[32,512,128]{2,1,0:T(8,128)(2,1)}, u32[]{:S(2)}) copy-start(bf16[32,512,128]{2,1,0:T(8,128)(2,1)} %param.20) | copy-start | bytes 12582916
  147.9 57.5 %reduce-scatter.2.cloned.1.call-start = ((), (), s32[]{:S(2)}) async-start(), calls=%async_computation.2 | async-start | bytes 1146880 | tf_op jit(solution)/shard_map/reduce_scatter | solution.py:445
Sparse Core Ops, SparseCore 0:
  148.0 21.3 all-gather.1
  180.3 25.0 reduce-scatter.1

commit v2 on v1

--- a/solution.py
+++ b/solution.py
@@ -340,6 +340,307 @@
     )(prompt_states, new_states, down_kv, gain_kv[None, :], cosine, sine)
 
 
+TOKENS = 4
+
+
+def attend_kernel(start_ref, low_ref, len_ref, ql_ref, qr_ref, bias_ref, cache_ref, new_ref, out_ref):
+    tokens = start_ref.shape[0]
+    nh = ql_ref.shape[0] // tokens
+    window = MAXLEN + 16
+    scale = 1.0 / math.sqrt(NOPE + ROPE)
+    contract = (((1,), (1,)), ((), ()))
+
+    def scores(content, turned, keys):
+        return (
+            lax.dot_general(content, keys[:, :KVL], contract, preferred_element_type=jnp.float32)
+            + lax.dot_general(turned, keys[:, KVL:], contract, preferred_element_type=jnp.float32)
+        ) * scale
+
+    def group(g, carry):
+        rows = pl.ds(pl.multiple_of(g * (TOKENS * nh), TOKENS * nh), TOKENS * nh)
+        content, turned = ql_ref[rows, :], qr_ref[rows, :]
+        score_new = scores(content, turned, new_ref[...])
+        held, weights_new = [], []
+        for i in range(TOKENS):
+            t = g * TOKENS + i
+            low = low_ref[t]
+            keys = cache_ref[pl.ds(pl.multiple_of(start_ref[t], 16), window), :]
+            mine = slice(i * nh, (i + 1) * nh)
+            score = scores(content[mine], turned[mine], keys)
+            column = lax.broadcasted_iota(jnp.int32, score.shape, 1)
+            usable = (column >= low) & (column < low + len_ref[t])
+            score = jnp.where(usable, score, -jnp.inf)
+            fresh = score_new[mine] + bias_ref[pl.ds(t, 1), :]
+            peak = jnp.maximum(
+                jnp.max(score, axis=1, keepdims=True), jnp.max(fresh, axis=1, keepdims=True)
+            )
+            score = jnp.exp(score - peak)
+            fresh = jnp.exp(fresh - peak)
+            total = jnp.sum(score, axis=1, keepdims=True) + jnp.sum(fresh, axis=1, keepdims=True)
+            weights_new.append(fresh / total)
+            held.append(
+                jnp.dot(
+                    (score / total).astype(jnp.bfloat16),
+                    keys[:, :KVL],
+                    preferred_element_type=jnp.float32,
+                )
+            )
+        mixed = jnp.dot(
+            jnp.concatenate(weights_new, axis=0).astype(jnp.bfloat16),
+            new_ref[:, :KVL],
+            preferred_element_type=jnp.float32,
+        )
+        out_ref[rows, :] = (jnp.concatenate(held, axis=0) + mixed).astype(jnp.bfloat16)
+        return carry
+
+    lax.fori_loop(0, tokens // TOKENS, group, 0)
+
+
+def attend(start, low, length, ql, qr, bias, cache, new_lat):
+    vmem = pl.BlockSpec(memory_space=pltpu.VMEM)
+    smem = pl.BlockSpec(memory_space=pltpu.SMEM)
+    return pl.pallas_call(
+        attend_kernel,
+        out_shape=jax.ShapeDtypeStruct(ql.shape, jnp.bfloat16),
+        in_specs=[smem] * 3 + [vmem] * 5,
+        out_specs=vmem,
+        compiler_params=pltpu.CompilerParams(vmem_limit_bytes=48 * 1024 * 1024),
+    )(start, low, length, ql, qr, bias, cache, new_lat)
+
+
+PIECES = 2
+
+
+def project_kernel(
+    heads,
+    seq,
+    tile,
+    ho_ref,
+    w_hbm,
+    out_ref,
+    w_ref,
+    gathered,
+    total,
+    out_buf,
+    from_left,
+    from_right,
+    w_sem,
+    x_send,
+    x_recv,
+    sib_send,
+    sib_recv,
+    rs_send,
+    rs_left,
+    rs_right,
+):
+    h = lax.axis_index("heads")
+    s = lax.axis_index("seq")
+    sibling = s + 1 - 2 * lax.rem(s, 2)
+    others = seq // 2 - 1
+    tokens, depth = ho_ref.shape
+    width = w_ref.shape[1]
+    tiles = width // tile
+    piece = tokens // PIECES
+    share = tokens * seq // heads
+
+    def fetch(n):
+        columns = pl.ds(n * tile, tile)
+        return pltpu.make_async_copy(w_hbm.at[:, columns], w_ref.at[:, columns], w_sem.at[n])
+
+    for n in range(tiles):
+        fetch(n).start()
+
+    barrier = pltpu.get_barrier_semaphore()
+
+    def greet(where):
+        pl.semaphore_signal(barrier, inc=1, device_id=where, device_id_type=MESH)
+
+    @pl.when(h > 0)
+    def _():
+        greet({"heads": h - 1})
+
+    @pl.when(h < heads - 1)
+    def _():
+        greet({"heads": h + 1})
+
+    greet({"seq": sibling})
+    for j in range(1, others + 1):
+        greet({"seq": lax.rem(s + 2 * j, seq)})
+    pl.semaphore_wait(
+        barrier,
+        1 + others + jnp.where(h > 0, 1, 0) + jnp.where(h < heads - 1, 1, 0),
+    )
+
+    def block(source, p):
+        return gathered.at[source, pl.ds(p * piece, piece), :]
+
+    def over(j, source, p):
+        return pltpu.make_async_remote_copy(
+            src_ref=ho_ref.at[pl.ds(p * piece, piece), :],
+            dst_ref=block(source, p),
+            send_sem=x_send.at[j - 1, p],
+            recv_sem=x_recv.at[j - 1, p],
+            device_id={"seq": lax.rem(s + 2 * j, seq)},
+            device_id_type=MESH,
+        )
+
+    def across(source, p, own):
+        return pltpu.make_async_remote_copy(
+            src_ref=ho_ref.at[pl.ds(p * piece, piece), :] if own else block(source, p),
+            dst_ref=block(source, p),
+            send_sem=sib_send.at[lax.div(source, 2), p],
+            recv_sem=sib_recv.at[lax.div(source, 2), p],
+            device_id={"seq": sibling},
+            device_id_type=MESH,
+        )
+
+    for p in range(PIECES):
+        for j in range(1, others + 1):
+            over(j, s, p).start()
+        across(s, p, True).start()
+    gathered[s] = ho_ref[...]
+    for p in range(PIECES):
+        for j in range(1, others + 1):
+            source = lax.rem(s - 2 * j + seq, seq)
+            over(j, source, p).wait_recv()
+            across(source, p, False).start()
+    for p in range(PIECES):
+        for j in range(others + 1):
+            across(lax.rem(sibling + 2 * j, seq), p, False).wait_recv()
+
+    for n in range(tiles):
+        fetch(n).wait()
+
+    for n in range(tiles):
+        rows = gathered[...].reshape(seq * tokens, depth)
+        total[:, n * tile : (n + 1) * tile] = jnp.dot(
+            rows, w_ref[:, n * tile : (n + 1) * tile], preferred_element_type=jnp.float32
+        )
+
+    def partial(c):
+        return total[pl.ds(pl.multiple_of(c * share, 16), share), :]
+
+    def send_right(c):
+        return pltpu.make_async_remote_copy(
+            src_ref=out_buf.at[c],
+            dst_ref=from_left.at[c],
+            send_sem=rs_send.at[c],
+            recv_sem=rs_left.at[c],
+            device_id={"heads": h + 1},
+            device_id_type=MESH,
+        )
+
+    def send_left(c):
+        return pltpu.make_async_remote_copy(
+            src_ref=out_buf.at[c],
+            dst_ref=from_right.at[c],
+            send_sem=rs_send.at[c],
+            recv_sem=rs_right.at[c],
+            device_id={"heads": h - 1},
+            device_id_type=MESH,
+        )
+
+    for i in range(heads - 1):
+        right, left = heads - 1 - i, i
+
+        @pl.when(h < right)
+        def _():
+            @pl.when(h == 0)
+            def _():
+                out_buf[right] = partial(right).astype(jnp.bfloat16)
+
+            @pl.when(h > 0)
+            def _():
+                send_right(right).wait_recv()
+                out_buf[right] = (
+                    partial(right) + from_left[right].astype(jnp.float32)
+                ).astype(jnp.bfloat16)
+
+            send_right(right).start()
+
+        @pl.when(h > left)
+        def _():
+            @pl.when(h == heads - 1)
+            def _():
+                out_buf[left] = partial(left).astype(jnp.bfloat16)
+
+            @pl.when(h < heads - 1)
+            def _():
+                send_left(left).wait_recv()
+                out_buf[left] = (
+                    partial(left) + from_right[left].astype(jnp.float32)
+                ).astype(jnp.bfloat16)
+
+            send_left(left).start()
+
+    @pl.when(h == 0)
+    def _():
+        send_left(h).wait_recv()
+        out_ref[...] = (partial(h) + from_right[h].astype(jnp.float32)).astype(jnp.bfloat16)
+
+    @pl.when(h == heads - 1)
+    def _():
+        send_right(h).wait_recv()
+        out_ref[...] = (partial(h) + from_left[h].astype(jnp.float32)).astype(jnp.bfloat16)
+
+    @pl.when((h > 0) & (h < heads - 1))
+    def _():
+        send_right(h).wait_recv()
+        send_left(h).wait_recv()
+        out_ref[...] = (
+            partial(h) + from_left[h].astype(jnp.float32) + from_right[h].astype(jnp.float32)
+        ).astype(jnp.bfloat16)
+
+    for c in range(heads):
+
+        @pl.when(h != c)
+        def _():
+            send_right(c).wait_send()
+
+    for p in range(PIECES):
+        for j in range(others + 1):
+            across(lax.rem(s + 2 * j, seq), p, False).wait_send()
+        for j in range(1, others + 1):
+            over(j, s, p).wait_send()
+
+
+def project(head_out, out_proj):
+    heads = lax.axis_size("heads")
+    seq = lax.axis_size("seq")
+    tokens, depth = head_out.shape
+    width = out_proj.shape[1]
+    tile = 256 if width % 256 == 0 else width
+    share = tokens * seq // heads
+    others = max(seq // 2 - 1, 1)
+    vmem = pl.BlockSpec(memory_space=pltpu.VMEM)
+    dma = pltpu.SemaphoreType.DMA
+    return pl.pallas_call(
+        functools.partial(project_kernel, heads, seq, tile),
+        out_shape=jax.ShapeDtypeStruct((share, width), jnp.bfloat16),
+        in_specs=[vmem, pl.BlockSpec(memory_space=pl.ANY)],
+        out_specs=vmem,
+        scratch_shapes=[
+            pltpu.VMEM((depth, width), jnp.bfloat16),
+            pltpu.VMEM((seq, tokens, depth), jnp.bfloat16),
+            pltpu.VMEM((seq * tokens, width), jnp.float32),
+            pltpu.VMEM((heads, share, width), jnp.bfloat16),
+            pltpu.VMEM((heads, share, width), jnp.bfloat16),
+            pltpu.VMEM((heads, share, width), jnp.bfloat16),
+            dma((width // tile,)),
+            dma((others, PIECES)),
+            dma((others, PIECES)),
+            dma((seq // 2, PIECES)),
+            dma((seq // 2, PIECES)),
+            dma((heads,)),
+            dma((heads,)),
+            dma((heads,)),
+        ],
+        compiler_params=pltpu.CompilerParams(
+            collective_id=1, has_side_effects=True, vmem_limit_bytes=56 * 1024 * 1024
+        ),
+    )(head_out, out_proj)
+
+
 def per_device(
     prompt_states,
     new_states,
@@ -396,55 +697,30 @@
     new_lat = new_lat[:dec_rows]
     prompt_lat = prompt_lat.reshape(owners * pr_rows, -1)
     slot_first = source * pr_rows + starts_all[source, slot_req]
-    offsets = jnp.arange(MAXLEN, dtype=jnp.int32)
-    softmax_scale = 1.0 / math.sqrt(NOPE + ROPE)
     query_latent = jnp.einsum(
         "thn,hnc->thc", queries[:, :, :NOPE], absorb_k, preferred_element_type=jnp.float32
     ).astype(jnp.bfloat16)
-    query_full = jnp.concatenate([query_latent, queries[:, :, NOPE:]], axis=2)
     row_first = slot_first[row_request]
-    row_cache = prompt_lat[
-        jnp.clip(row_first[:, None] + offsets[None, :], 0, owners * pr_rows - 1)
-    ]
-    cache_pos = jnp.arange(row_cache.shape[1], dtype=jnp.int32)
-    score_cache = (
-        jnp.einsum("thc,tpc->thp", query_full, row_cache, preferred_element_type=jnp.float32)
-        * softmax_scale
-    )
-    score_new = (
-        jnp.einsum("thc,uc->thu", query_full, new_lat, preferred_element_type=jnp.float32)
-        * softmax_scale
-    )
-    ok_cache = (cache_pos[None, :] < row_len[:, None])[:, None, :]
-    ok_new = (same_slot & (token_ids[None, :] <= token_ids[:, None]))[:, None, :]
-    peak_score = jnp.maximum(
-        jnp.max(jnp.where(ok_cache, score_cache, -jnp.inf), axis=2),
-        jnp.max(jnp.where(ok_new, score_new, -jnp.inf), axis=2),
-    )
-    exp_cache = jnp.where(ok_cache, jnp.exp(score_cache - peak_score[:, :, None]), 0.0)
-    exp_new = jnp.where(ok_new, jnp.exp(score_new - peak_score[:, :, None]), 0.0)
-    denominator = jnp.sum(exp_cache, axis=2) + jnp.sum(exp_new, axis=2)
-    weight_cache = (exp_cache / denominator[:, :, None]).astype(jnp.bfloat16)
-    weight_new = (exp_new / denominator[:, :, None]).astype(jnp.bfloat16)
-    latent_out = jnp.einsum(
-        "thp,tpc->thc", weight_cache, row_cache[:, :, :KVL], preferred_element_type=jnp.float32
-    )
-    latent_out = latent_out + jnp.einsum(
-        "thu,uc->thc", weight_new, new_lat[:, :KVL], preferred_element_type=jnp.float32
-    )
-    latent_out = latent_out.astype(jnp.bfloat16)
+    start = jnp.minimum(row_first // 16 * 16, owners * pr_rows - (MAXLEN + 16))
+    bias = jnp.where(
+        same_slot & (token_ids[None, :] <= token_ids[:, None]), jnp.float32(0), -jnp.inf
+    )
+    local_heads = queries.shape[1]
+    latent_out = attend(
+        start,
+        row_first - start,
+        row_len,
+        query_latent.reshape(dec_rows * local_heads, KVL),
+        queries[:, :, NOPE:].reshape(dec_rows * local_heads, ROPE),
+        bias,
+        prompt_lat,
+        new_lat,
+    ).reshape(dec_rows, local_heads, KVL)
     head_out = jnp.einsum(
         "thc,hcv->thv", latent_out, absorb_v, preferred_element_type=jnp.float32
     ).astype(jnp.bfloat16)
     head_out = head_out.reshape(dec_rows, -1)
-    projected = jnp.dot(
-        lax.all_gather(head_out, "seq", axis=0, tiled=True),
-        out_proj,
-        preferred_element_type=jnp.float32,
-    )
-    return lax.psum_scatter(
-        projected.astype(jnp.bfloat16), "heads", scatter_dimension=0, tiled=True
-    )
+    return project(head_out, out_proj)
 
 
 def solution(mesh):

time: 213 us -> 165 us (0.77)
  Pallas kernels: 59.7 us -> 142 us
  waiting for transfers between devices: 46.6 us -> 0 us
  local copies, waits for them, and re-layouts: 51.5 us -> 13.2 us
  matrix products: 31.8 us -> 5.51 us
  between operations: 13.6 us -> 0.2 us
  other arithmetic: 8.83 us -> 4.07 us
    pallas_call x0 -> x2, Pallas kernels: none -> 81.9 us  [the longest x1 48.8 us: project(): pl.pallas_call(functools.partial(project_kernel, heads, seq, tile), out_s...]
    gather x1 -> x0, local copies, waits for them, and re-layouts: 37.6 us -> none  [per_device(): prompt_lat[jnp.clip(row_first[:, None] + offsets[None, :], 0, owners * pr...]
    dot_general x5 -> x0, matrix products: 26.3 us -> none  [the longest x1 10.7 us: per_device(): jnp.dot(lax.all_gather(head_out, 'seq', axis=0, tiled=True), out_proj, pr...]
    reduce_scatter x1 -> x0, waiting for transfers between devices: 25.3 us -> none  [per_device(): lax.psum_scatter(projected.astype(jnp.bfloat16), 'heads', scatter_dimensi...]
    all_gather x1 -> x0, waiting for transfers between devices: 21.3 us -> none  [per_device(): lax.all_gather(head_out, 'seq', axis=0, tiled=True)]
    reduce_sum x2 -> x0, other arithmetic: 2.13 us -> none  [per_device(): denominator = jnp.sum(exp_cache, axis=2) + jnp.sum(exp_new, axis=2)]
    unnamed x14 -> x16, local copies, waits for them, and re-layouts: 7.43 us -> 6.59 us
  transfers between devices with their start and end apart: 2 -> 0, of which waited for: 2 -> 0; matrix products, arithmetic and copies ran while one was open for 0% -> 0% of each run, Pallas kernels for 0% -> 0%
where the time goes in v2:
time: 165 us
  Pallas kernels  142 us (86%)
  local copies, waits for them, and re-layouts  13.2 us (8%)
  matrix products  5.51 us (3%)
  other arithmetic  4.07 us (2%)
    pallas_call x1, Pallas kernels, latent_rows(): pl.pallas_call(functools.partial(latent_kernel, heads, seq), out_shape=(j...  59.6 us
    pallas_call x1, Pallas kernels, project(): pl.pallas_call(functools.partial(project_kernel, heads, seq, tile), out_s...  48.8 us
    pallas_call x1, Pallas kernels, attend(): pl.pallas_call(attend_kernel, out_shape=jax.ShapeDtypeStruct(ql.shape, jn...  33.1 us
    unnamed x16, local copies, waits for them, and re-layouts  6.59 us

profile of v2, /device:TPU:0, one launch (start us, length us, event | category | flops | bytes accessed | tf_op | source)
XLA Modules:
  0.0 164.6 jit_solution(9846935642940599576)
XLA Ops:
  0.0 0.0 copy-start
  0.0 0.0 copy-start.3
  0.0 0.0 copy-start.2
  0.0 0.9 reduce_window_sum.11
  0.9 0.7 sub.24
  1.6 0.1 select_reduce_fusion
  1.7 0.1 dynamic_slice.10
  1.8 0.0 copy-done
  1.8 0.7 gather_fusion
  2.5 1.4 gather_fusion.3
  3.9 0.7 compare_select_fusion
  4.6 0.8 gather_fusion.4
  5.3 0.9 convert_reduce_fusion
  6.3 0.1 dynamic_slice.11
  6.3 0.1 add_convert_fusion
  6.4 0.5 fusion.9
  6.9 0.1 pad_maximum_fusion
  7.0 3.1 %copy.30.w_ref = bf16[1792,576]{1,0:T(8,128)(2,1)S(1)} copy(bf16[1792,576]{0,1:T(8,128)(2,1)} %param.18) | data formatting | bytes 4128768 | tf_op args[7]
  10.2 0.0 copy-done.3
  10.2 0.0 copy-done.2
  10.2 0.0 copy-start.1
  10.2 1.8 %copy-done.1 = bf16[768,1792]{1,0:T(8,128)(2,1)S(1)} copy-done((bf16[768,1792]{1,0:T(8,128)(2,1)S(1)}, bf16[768,1792]{1,0:T(8,128)(2,1)}, u32[]{:S(2)}) %copy-start.1) | copy-done | bytes 2752536
  12.0 0.0 slice-start
  12.0 59.6 %shard_map.109 = (bf16[4,768,576]{2,1,0:T(8,128)(2,1)}, bf16[64,576]{1,0:T(8,128)(2,1)S(1)}) custom-call(bf16[768,1792]{1,0:T(8,128)(2,1)S(1)} %copy-done.1, bf16[64,1792]{1,0:T(8,128)(2,1)S(1)} %copy-done.2, bf16[1792,576]{1,0:T(8,128)(2,1)S(1)} %copy.30.w_ref, f32[1,512]{1,0:T(1,128)S(1)} %bitcast.28, f32[208,64]{1,0:T(8,128)S(1)} %get-tuple-element.14.cos_ref, ...), custom_call_target="tpu_custom_call" | custom-call | tf_op jit(solution)/shard_map/pallas_call | solution.py:314
  71.6 0.7 gather_fusion.1
  72.3 0.8 gather_fusion.2
  73.1 0.0 slice-done
  73.1 0.0 copy-start.5
  73.2 3.0 %convert_bitcast_fusion = bf16[64,32,512]{2,0,1:T(8,128)(2,1)S(1)} fusion(bf16[32,128,512]{2,1,0:T(8,128)(2,1)} %param.19, bf16[64,32,128]{2,1,0:T(8,128)(2,1)S(1)} %slice-done), kind=kOutput, calls=%fused_computation.7 | convolution fusion | flops 269484032 | bytes 6815744 | tf_op jit(solution)/shard_map/thn,hnc->thc/dot_general | solution.py:700
  76.1 0.0 copy-start.6
  76.2 1.2 copy.28
  77.3 0.0 copy-done.5
  77.3 0.1 slice.7
  77.4 0.0 copy-done.6
  77.5 0.1 fusion.10.bias_ref
  77.5 0.0 copy-start.4
  77.5 33.1 %shard_map.110 = bf16[2048,512]{1,0:T(8,128)(2,1)S(1)} custom-call(s32[64]{0:T(128)S(1)} %get-tuple-element.10.start_ref, s32[64]{0:T(128)S(1)} %get-tuple-element.9.low_ref, s32[64]{0:T(128)S(1)} %gather_fusion.4, bf16[2048,512]{1,0:T(8,128)(2,1)S(1)} %bitcast.25, bf16[2048,64]{1,0:T(8,128)(2,1)S(1)} %bitcast.27, f32[64,64]{1,0:T(8,128)S(1)} %fusion.10.bias_ref, ...), custom_call_target="tpu_custom_call" | custom-call | tf_op jit(solution)/shard_map/pallas_call | solution.py:402
  110.7 0.0 copy-done.4
  110.7 2.5 %fusion.5 = bf16[32,8,8,128]{3,2,1,0:T(8,128)(2,1)S(1)} fusion(bf16[32,512,128]{2,1,0:T(8,128)(2,1)S(1)} %copy-done.4, bf16[64,32,512]{2,1,0:T(8,128)(2,1)S(1)} %bitcast.26), kind=kOutput, calls=%fused_computation.9 | convolution fusion | flops 268697600 | bytes 6815744 | tf_op jit(solution)/shard_map/thc,hcv->thv/dot_general | solution.py:719
  113.2 0.9 copy.44
  114.1 48.8 %shard_map.111 = bf16[64,1792]{1,0:T(8,128)(2,1)} custom-call(bf16[64,4096]{1,0:T(8,128)(2,1)} %bitcast.30, bf16[4096,1792]{1,0:T(8,128)(2,1)} %w_hbm.1), custom_call_target="tpu_custom_call" | custom-call | tf_op jit(solution)/shard_map/pallas_call | solution.py:617
  162.9 1.6 copy.46
  (9 shorter events, 0.1 us)
Async XLA Ops:
  0.0 1.8 %copy-start = (s32[4,16]{1,0:T(4,128)S(1)}, s32[4,16]{1,0:T(4,128)}, u32[]{:S(2)}) copy-start(s32[4,16]{1,0:T(4,128)} %param.14) | copy-start | bytes 772
  0.0 10.2 %copy-start.3 = (f32[512]{0:T(512)S(1)}, f32[512]{0:T(512)}, u32[]{:S(2)}) copy-start(f32[512]{0:T(512)} %param.17) | copy-start | bytes 6148
  0.0 10.2 %copy-start.2 = (bf16[64,1792]{1,0:T(8,128)(2,1)S(1)}, bf16[64,1792]{1,0:T(8,128)(2,1)}, u32[]{:S(2)}) copy-start(bf16[64,1792]{1,0:T(8,128)(2,1)} %n_ref.1) | copy-start | bytes 688132
  10.2 1.8 %copy-start.1 = (bf16[768,1792]{1,0:T(8,128)(2,1)S(1)}, bf16[768,1792]{1,0:T(8,128)(2,1)}, u32[]{:S(2)}) copy-start(bf16[768,1792]{1,0:T(8,128)(2,1)} %x_ref.1) | copy-start | bytes 8257540
  12.0 61.2 %slice-start = ((bf16[64,32,192]{2,1,0:T(8,128)(2,1)}), bf16[64,32,128]{2,1,0:T(8,128)(2,1)S(1)}, s32[]{:S(2)}) async-start(bf16[64,32,192]{2,1,0:T(8,128)(2,1)} %param.16), calls=%async_computation | async-start | bytes 1048576 | tf_op jit(solution)/shard_map/slice | solution.py:701
  73.1 4.2 %copy-start.5 = (bf16[64,32,192]{2,1,0:T(8,128)(2,1)S(1)}, bf16[64,32,192]{2,1,0:T(8,128)(2,1)}, u32[]{:S(2)}) copy-start(bf16[64,32,192]{2,1,0:T(8,128)(2,1)} %param.16) | copy-start | bytes 2359300
  76.1 1.3 copy-start.6
  77.5 33.1 %copy-start.4 = (bf16[32,512,128]{2,1,0:T(8,128)(2,1)S(1)}, bf16[32,512,128]{2,1,0:T(8,128)(2,1)}, u32[]{:S(2)}) copy-start(bf16[32,512,128]{2,1,0:T(8,128)(2,1)} %param.20) | copy-start | bytes 12582916

commit v3 on v2

--- a/solution.py
+++ b/solution.py
@@ -83,11 +83,16 @@
         1 + others + jnp.where(h > 0, 1, 0) + jnp.where(h < heads - 1, 1, 0),
     )
 
-    new_part[...] = jnp.dot(n_ref[...], w_ref[...], preferred_element_type=jnp.float32)
+    def compress(rows):
+        return lax.dot_general(
+            rows, w_ref[...], (((1,), (1,)), ((), ())), preferred_element_type=jnp.float32
+        )
+
+    new_part[...] = compress(n_ref[...])
 
     def partial(c):
         rows = x_ref[pl.ds(pl.multiple_of(c * cp, 16), cp), :]
-        top = jnp.dot(rows, w_ref[...], preferred_element_type=jnp.float32)
+        top = compress(rows)
         return jnp.concatenate([top, new_part[pl.ds(pl.multiple_of(c * pn, 16), pn), :]], axis=0)
 
     def send_right(c):
@@ -337,10 +342,10 @@
         compiler_params=pltpu.CompilerParams(
             collective_id=0, has_side_effects=True, vmem_limit_bytes=48 * 1024 * 1024
         ),
-    )(prompt_states, new_states, down_kv, gain_kv[None, :], cosine, sine)
-
-
-TOKENS = 4
+    )(prompt_states, new_states, down_kv.T, gain_kv[None, :], cosine, sine)
+
+
+TOKENS = 16
 
 
 def attend_kernel(start_ref, low_ref, len_ref, ql_ref, qr_ref, bias_ref, cache_ref, new_ref, out_ref):
@@ -359,34 +364,35 @@
     def group(g, carry):
         rows = pl.ds(pl.multiple_of(g * (TOKENS * nh), TOKENS * nh), TOKENS * nh)
         content, turned = ql_ref[rows, :], qr_ref[rows, :]
-        score_new = scores(content, turned, new_ref[...])
-        held, weights_new = [], []
+        spans = [slice(i * nh, (i + 1) * nh) for i in range(TOKENS)]
+        column = lax.broadcasted_iota(jnp.int32, (nh, window), 1)
+        keys, score, bias = [], [], []
         for i in range(TOKENS):
             t = g * TOKENS + i
             low = low_ref[t]
-            keys = cache_ref[pl.ds(pl.multiple_of(start_ref[t], 16), window), :]
-            mine = slice(i * nh, (i + 1) * nh)
-            score = scores(content[mine], turned[mine], keys)
-            column = lax.broadcasted_iota(jnp.int32, score.shape, 1)
+            keys.append(cache_ref[pl.ds(pl.multiple_of(start_ref[t], 16), window), :])
             usable = (column >= low) & (column < low + len_ref[t])
-            score = jnp.where(usable, score, -jnp.inf)
-            fresh = score_new[mine] + bias_ref[pl.ds(t, 1), :]
-            peak = jnp.maximum(
-                jnp.max(score, axis=1, keepdims=True), jnp.max(fresh, axis=1, keepdims=True)
+            score.append(
+                jnp.where(usable, scores(content[spans[i]], turned[spans[i]], keys[i]), -jnp.inf)
             )
-            score = jnp.exp(score - peak)
-            fresh = jnp.exp(fresh - peak)
-            total = jnp.sum(score, axis=1, keepdims=True) + jnp.sum(fresh, axis=1, keepdims=True)
-            weights_new.append(fresh / total)
-            held.append(
-                jnp.dot(
-                    (score / total).astype(jnp.bfloat16),
-                    keys[:, :KVL],
-                    preferred_element_type=jnp.float32,
-                )
-            )
+            bias.append(jnp.broadcast_to(bias_ref[pl.ds(t, 1), :], (nh, tokens)))
+        score = jnp.concatenate(score, axis=0)
+        fresh = scores(content, turned, new_ref[...]) + jnp.concatenate(bias, axis=0)
+        peak = jnp.maximum(
+            jnp.max(score, axis=1, keepdims=True), jnp.max(fresh, axis=1, keepdims=True)
+        )
+        score = jnp.exp(score - peak)
+        fresh = jnp.exp(fresh - peak)
+        inverse = 1.0 / (
+            jnp.sum(score, axis=1, keepdims=True) + jnp.sum(fresh, axis=1, keepdims=True)
+        )
+        weights = (score * inverse).astype(jnp.bfloat16)
+        held = [
+            jnp.dot(weights[span], key[:, :KVL], preferred_element_type=jnp.float32)
+            for span, key in zip(spans, keys)
+        ]
         mixed = jnp.dot(
-            jnp.concatenate(weights_new, axis=0).astype(jnp.bfloat16),
+            (fresh * inverse).astype(jnp.bfloat16),
             new_ref[:, :KVL],
             preferred_element_type=jnp.float32,
         )
@@ -415,6 +421,7 @@
     heads,
     seq,
     tile,
+    spans,
     ho_ref,
     w_hbm,
     out_ref,
@@ -508,94 +515,104 @@
         for j in range(others + 1):
             across(lax.rem(sibling + 2 * j, seq), p, False).wait_recv()
 
-    for n in range(tiles):
-        fetch(n).wait()
-
-    for n in range(tiles):
-        rows = gathered[...].reshape(seq * tokens, depth)
-        total[:, n * tile : (n + 1) * tile] = jnp.dot(
-            rows, w_ref[:, n * tile : (n + 1) * tile], preferred_element_type=jnp.float32
-        )
-
-    def partial(c):
-        return total[pl.ds(pl.multiple_of(c * share, 16), share), :]
-
-    def send_right(c):
+    def cut(q):
+        return pl.ds(spans[q][0], spans[q][1])
+
+    def partial(c, q):
+        return total[pl.ds(pl.multiple_of(c * share, 16), share), cut(q)]
+
+    def send_right(c, q):
         return pltpu.make_async_remote_copy(
-            src_ref=out_buf.at[c],
-            dst_ref=from_left.at[c],
-            send_sem=rs_send.at[c],
-            recv_sem=rs_left.at[c],
+            src_ref=out_buf.at[c, :, cut(q)],
+            dst_ref=from_left.at[c, :, cut(q)],
+            send_sem=rs_send.at[c, q],
+            recv_sem=rs_left.at[c, q],
             device_id={"heads": h + 1},
             device_id_type=MESH,
         )
 
-    def send_left(c):
+    def send_left(c, q):
         return pltpu.make_async_remote_copy(
-            src_ref=out_buf.at[c],
-            dst_ref=from_right.at[c],
-            send_sem=rs_send.at[c],
-            recv_sem=rs_right.at[c],
+            src_ref=out_buf.at[c, :, cut(q)],
+            dst_ref=from_right.at[c, :, cut(q)],
+            send_sem=rs_send.at[c, q],
+            recv_sem=rs_right.at[c, q],
             device_id={"heads": h - 1},
             device_id_type=MESH,
         )
 
-    for i in range(heads - 1):
-        right, left = heads - 1 - i, i
-
-        @pl.when(h < right)
-        def _():
-            @pl.when(h == 0)
+    for q, (low, size) in enumerate(spans):
+        for n in range(low // tile, (low + size) // tile):
+            fetch(n).wait()
+            rows = gathered[...].reshape(seq * tokens, depth)
+            total[:, n * tile : (n + 1) * tile] = jnp.dot(
+                rows, w_ref[:, n * tile : (n + 1) * tile], preferred_element_type=jnp.float32
+            )
+
+        @pl.when(h == 0)
+        def _():
+            for c in range(heads - 1, 0, -1):
+                out_buf[c, :, cut(q)] = partial(c, q).astype(jnp.bfloat16)
+                send_right(c, q).start()
+
+        @pl.when(h == heads - 1)
+        def _():
+            for c in range(heads - 1):
+                out_buf[c, :, cut(q)] = partial(c, q).astype(jnp.bfloat16)
+                send_left(c, q).start()
+
+    for q in range(len(spans)):
+        for i in range(heads - 1):
+            right, left = heads - 1 - i, i
+
+            @pl.when((h > 0) & (h < right))
             def _():
-                out_buf[right] = partial(right).astype(jnp.bfloat16)
-
-            @pl.when(h > 0)
+                send_right(right, q).wait_recv()
+                out_buf[right, :, cut(q)] = (
+                    partial(right, q) + from_left[right, :, cut(q)].astype(jnp.float32)
+                ).astype(jnp.bfloat16)
+                send_right(right, q).start()
+
+            @pl.when((h > left) & (h < heads - 1))
             def _():
-                send_right(right).wait_recv()
-                out_buf[right] = (
-                    partial(right) + from_left[right].astype(jnp.float32)
+                send_left(left, q).wait_recv()
+                out_buf[left, :, cut(q)] = (
+                    partial(left, q) + from_right[left, :, cut(q)].astype(jnp.float32)
                 ).astype(jnp.bfloat16)
-
-            send_right(right).start()
-
-        @pl.when(h > left)
-        def _():
-            @pl.when(h == heads - 1)
-            def _():
-                out_buf[left] = partial(left).astype(jnp.bfloat16)
-
-            @pl.when(h < heads - 1)
-            def _():
-                send_left(left).wait_recv()
-                out_buf[left] = (
-                    partial(left) + from_right[left].astype(jnp.float32)
-                ).astype(jnp.bfloat16)
-
-            send_left(left).start()
-
-    @pl.when(h == 0)
-    def _():
-        send_left(h).wait_recv()
-        out_ref[...] = (partial(h) + from_right[h].astype(jnp.float32)).astype(jnp.bfloat16)
-
-    @pl.when(h == heads - 1)
-    def _():
-        send_right(h).wait_recv()
-        out_ref[...] = (partial(h) + from_left[h].astype(jnp.float32)).astype(jnp.bfloat16)
-
-    @pl.when((h > 0) & (h < heads - 1))
-    def _():
-        send_right(h).wait_recv()
-        send_left(h).wait_recv()
-        out_ref[...] = (
-            partial(h) + from_left[h].astype(jnp.float32) + from_right[h].astype(jnp.float32)
-        ).astype(jnp.bfloat16)
+                send_left(left, q).start()
+
+    for q in range(len(spans)):
+
+        @pl.when(h == 0)
+        def _():
+            send_left(h, q).wait_recv()
+            out_ref[:, cut(q)] = (
+                partial(h, q) + from_right[h, :, cut(q)].astype(jnp.float32)
+            ).astype(jnp.bfloat16)
+
+        @pl.when(h == heads - 1)
+        def _():
+            send_right(h, q).wait_recv()
+            out_ref[:, cut(q)] = (
+                partial(h, q) + from_left[h, :, cut(q)].astype(jnp.float32)
+            ).astype(jnp.bfloat16)
+
+        @pl.when((h > 0) & (h < heads - 1))
+        def _():
+            send_right(h, q).wait_recv()
+            send_left(h, q).wait_recv()
+            out_ref[:, cut(q)] = (
+                partial(h, q)
+                + from_left[h, :, cut(q)].astype(jnp.float32)
+                + from_right[h, :, cut(q)].astype(jnp.float32)
+            ).astype(jnp.bfloat16)
 
     for c in range(heads):
 
         @pl.when(h != c)
         def _():
-            send_right(c).wait_send()
+            for q in range(len(spans)):
+                send_right(c, q).wait_send()
 
     for p in range(PIECES):
         for j in range(others + 1):
@@ -610,12 +627,14 @@
     tokens, depth = head_out.shape
     width = out_proj.shape[1]
     tile = 256 if width % 256 == 0 else width
+    middle = (width // tile + 1) // 2 * tile
+    spans = [(0, middle), (middle, width - middle)] if middle < width else [(0, width)]
     share = tokens * seq // heads
     others = max(seq // 2 - 1, 1)
     vmem = pl.BlockSpec(memory_space=pltpu.VMEM)
     dma = pltpu.SemaphoreType.DMA
     return pl.pallas_call(
-        functools.partial(project_kernel, heads, seq, tile),
+        functools.partial(project_kernel, heads, seq, tile, spans),
         out_shape=jax.ShapeDtypeStruct((share, width), jnp.bfloat16),
         in_specs=[vmem, pl.BlockSpec(memory_space=pl.ANY)],
         out_specs=vmem,
@@ -631,9 +650,9 @@
             dma((others, PIECES)),
             dma((seq // 2, PIECES)),
             dma((seq // 2, PIECES)),
-            dma((heads,)),
-            dma((heads,)),
-            dma((heads,)),
+            dma((heads, len(spans))),
+            dma((heads, len(spans))),
+            dma((heads, len(spans))),
         ],
         compiler_params=pltpu.CompilerParams(
             collective_id=1, has_side_effects=True, vmem_limit_bytes=56 * 1024 * 1024
@@ -660,33 +679,49 @@
     per_peer = requests // owners
     pr_rows = prompt_states.shape[0]
     dec_rows = new_states.shape[0]
-    starts_all = jnp.cumsum(prompt_lengths, axis=1) - prompt_lengths
-    my_lengths = prompt_lengths[own_index]
-    my_starts = starts_all[own_index]
-    row_ids = jnp.arange(pr_rows, dtype=jnp.int32)
-    row_start = jnp.max(
-        jnp.where(my_starts[None, :] <= row_ids[:, None], my_starts[None, :], 0), axis=1
-    )
-    prompt_pos = row_ids - row_start
-    slot_ids = jnp.arange(requests, dtype=jnp.int32)
-    source = slot_ids // per_peer
-    slot_req = routing[source, own_index * per_peer + slot_ids % per_peer]
-    slot_len = prompt_lengths[source, slot_req]
-    token_ids = jnp.arange(dec_rows, dtype=jnp.int32)
-    same_slot = row_request[:, None] == row_request[None, :]
-    earlier = jnp.sum(
-        (same_slot & (token_ids[:, None] > token_ids[None, :])).astype(jnp.int32), axis=1
-    )
-    row_len = slot_len[row_request]
-    new_pos = row_len + earlier
     heads = lax.axis_size("heads")
     head_index = lax.axis_index("heads")
     cp = pr_rows // heads
     pn = 16 * -(-dec_rows // (16 * heads))
     padded = pn * heads - dec_rows
+    request_ids = jnp.arange(requests, dtype=jnp.int32)
+    starts_all = jnp.sum(
+        jnp.where(
+            request_ids[None, None, :] < request_ids[None, :, None],
+            prompt_lengths[:, None, :],
+            0,
+        ),
+        axis=2,
+    )
+    my_starts = lax.dynamic_slice_in_dim(starts_all, own_index, 1)
+    row_ids = head_index * cp + jnp.arange(cp, dtype=jnp.int32)
+    row_start = jnp.max(
+        jnp.where(my_starts <= row_ids[:, None], my_starts, 0), axis=1
+    )
+    prompt_pos = row_ids - row_start
+    source = request_ids // per_peer
+    slot_req = lax.dynamic_slice_in_dim(
+        routing.reshape(owners, owners, per_peer), own_index, 1, axis=1
+    ).reshape(requests)
+    chosen = slot_req[:, None] == request_ids[None, :]
+    slot_len = jnp.sum(
+        jnp.where(chosen, jnp.repeat(prompt_lengths, per_peer, axis=0), 0), axis=1
+    )
+    slot_first = source * pr_rows + jnp.sum(
+        jnp.where(chosen, jnp.repeat(starts_all, per_peer, axis=0), 0), axis=1
+    )
+    token_ids = jnp.arange(dec_rows, dtype=jnp.int32)
+    same_slot = row_request[:, None] == row_request[None, :]
+    earlier = jnp.sum(
+        (same_slot & (token_ids[:, None] > token_ids[None, :])).astype(jnp.int32), axis=1
+    )
+    row_slot = row_request[:, None] == request_ids[None, :]
+    row_len = jnp.sum(jnp.where(row_slot, slot_len[None, :], 0), axis=1)
+    row_first = jnp.sum(jnp.where(row_slot, slot_first[None, :], 0), axis=1)
+    new_pos = row_len + earlier
     my_pos = jnp.concatenate(
         [
-            lax.dynamic_slice_in_dim(prompt_pos, head_index * cp, cp),
+            prompt_pos,
             lax.dynamic_slice_in_dim(jnp.pad(new_pos, (0, padded)), head_index * pn, pn),
         ]
     )
@@ -696,11 +731,9 @@
     )
     new_lat = new_lat[:dec_rows]
     prompt_lat = prompt_lat.reshape(owners * pr_rows, -1)
-    slot_first = source * pr_rows + starts_all[source, slot_req]
     query_latent = jnp.einsum(
         "thn,hnc->thc", queries[:, :, :NOPE], absorb_k, preferred_element_type=jnp.float32
     ).astype(jnp.bfloat16)
-    row_first = slot_first[row_request]
     start = jnp.minimum(row_first // 16 * 16, owners * pr_rows - (MAXLEN + 16))
     bias = jnp.where(
         same_slot & (token_ids[None, :] <= token_ids[:, None]), jnp.float32(0), -jnp.inf

time: 165 us -> 140 us (0.85)
  Pallas kernels: 142 us -> 122 us
  local copies, waits for them, and re-layouts: 13.2 us -> 6.92 us
    pallas_call x1, Pallas kernels: 33.1 us -> 11.7 us  [attend(): pl.pallas_call(attend_kernel, out_shape=jax.ShapeDtypeStruct(ql.shape, jn...]
    unnamed x16 -> x11, local copies, waits for them, and re-layouts: 6.59 us -> 1.67 us
    gather x5 -> x0, local copies, waits for them, and re-layouts: 4.29 us -> none  [the longest x1 1.37 us: per_device(): slot_len = prompt_lengths[source, slot_req]]
    reduce_sum x0 -> x3, other arithmetic: none -> 2.54 us  [the longest x1 0.97 us: per_device(): jnp.sum(jnp.where(chosen, jnp.repeat(prompt_lengths, per_peer, axis=0), 0...]
where the time goes in v3:
time: 140 us
  Pallas kernels  122 us (87%)
  local copies, waits for them, and re-layouts  6.92 us (5%)
  matrix products  5.6 us (4%)
  other arithmetic  5.05 us (4%)
    pallas_call x1, Pallas kernels, latent_rows(): pl.pallas_call(functools.partial(latent_kernel, heads, seq), out_shape=(j...  60.3 us
    pallas_call x1, Pallas kernels, project(): pl.pallas_call(functools.partial(project_kernel, heads, seq, tile, spans)...  49.9 us
    pallas_call x1, Pallas kernels, attend(): pl.pallas_call(attend_kernel, out_shape=jax.ShapeDtypeStruct(ql.shape, jn...  11.7 us
    dot_general x1, matrix products, per_device(): jnp.einsum('thn,hnc->thc', queries[:, :, :NOPE], absorb_k, preferred_elem...  3.08 us

profile of v3, /device:TPU:0, one launch (start us, length us, event | category | flops | bytes accessed | tf_op | source)
XLA Modules:
  0.0 139.7 jit_solution(15601798383462293746)
XLA Ops:
  0.0 0.9 convert_reduce_fusion
  1.0 0.8 select_reduce_fusion
  1.8 0.1 select_reduce_fusion.1
  1.9 0.8 reshape.103
  2.7 1.0 select_reduce_fusion.3
  3.6 0.1 broadcast_in_dim.97
  3.7 0.1 reduce_sum.58
  3.8 0.8 select_reduce_fusion.2
  4.6 0.1 dynamic_slice.11
  4.7 0.1 add_convert_fusion
  4.8 0.8 fusion.10.bias_ref
  5.6 0.4 fusion.9
  6.0 0.1 pad_maximum_fusion
  6.1 1.1 slice.7
  7.2 1.1 slice.6
  8.3 0.0 copy-start
  8.3 0.0 copy-start.1
  8.3 0.0 copy-start.2
  8.3 0.0 copy-start.3
  8.4 3.1 %convert_bitcast_fusion = bf16[64,32,512]{2,0,1:T(8,128)(2,1)S(1)} fusion(bf16[32,128,512]{2,1,0:T(8,128)(2,1)} %param.19, bf16[64,32,128]{2,1,0:T(8,128)(2,1)S(1)} %slice.6), kind=kOutput, calls=%fused_computation.2 | convolution fusion | flops 269484032 | bytes 6815744 | tf_op jit(solution)/shard_map/thn,hnc->thc/dot_general | solution.py:734
  11.4 1.2 copy.21
  12.6 0.0 copy-done
  12.6 0.0 copy-done.1
  12.6 0.0 copy-done.2
  12.6 0.0 copy-done.3
  12.7 60.3 %shard_map.109 = (bf16[4,768,576]{2,1,0:T(8,128)(2,1)}, bf16[64,576]{1,0:T(8,128)(2,1)S(1)}) custom-call(bf16[768,1792]{1,0:T(8,128)(2,1)S(1)} %copy-done, bf16[64,1792]{1,0:T(8,128)(2,1)S(1)} %copy-done.2, bf16[576,1792]{1,0:T(8,128)(2,1)S(1)} %bitcast.22, f32[1,512]{1,0:T(1,128)S(1)} %bitcast.23, f32[208,64]{1,0:T(8,128)S(1)} %get-tuple-element.18.cos_ref, ...), custom_call_target="tpu_custom_call" | custom-call | tf_op jit(solution)/shard_map/pallas_call | solution.py:319
  73.0 0.0 copy-start.4
  73.0 11.7 %shard_map.110 = bf16[2048,512]{1,0:T(8,128)(2,1)S(1)} custom-call(s32[64]{0:T(128)S(1)} %get-tuple-element.14.start_ref, s32[64]{0:T(128)S(1)} %get-tuple-element.13.low_ref, s32[64]{0:T(128)S(1)} %get-tuple-element.11.len_ref, bf16[2048,512]{1,0:T(8,128)(2,1)S(1)} %bitcast.19, bf16[2048,64]{1,0:T(8,128)(2,1)S(1)} %bitcast.21, ...), custom_call_target="tpu_custom_call" | custom-call | tf_op jit(solution)/shard_map/pallas_call | solution.py:408
  84.7 0.0 copy-done.4
  84.7 2.5 %fusion.5 = bf16[32,8,8,128]{3,2,1,0:T(8,128)(2,1)S(1)} fusion(bf16[32,512,128]{2,1,0:T(8,128)(2,1)S(1)} %copy-done.4, bf16[64,32,512]{2,1,0:T(8,128)(2,1)S(1)} %bitcast.20), kind=kOutput, calls=%fused_computation.4 | convolution fusion | flops 268697600 | bytes 6815744 | tf_op jit(solution)/shard_map/thc,hcv->thv/dot_general | solution.py:752
  87.2 0.9 copy.36
  88.1 49.9 %shard_map.111 = bf16[64,1792]{1,0:T(8,128)(2,1)} custom-call(bf16[64,4096]{1,0:T(8,128)(2,1)} %bitcast.25, bf16[4096,1792]{1,0:T(8,128)(2,1)} %w_hbm.1), custom_call_target="tpu_custom_call" | custom-call | tf_op jit(solution)/shard_map/pallas_call | solution.py:636
  138.0 1.6 %copy.38 = bf16[64,1792]{1,0:T(8,128)(2,1)} copy(bf16[64,1792]{1,0:T(8,128)(2,1)} %shard_map.111) | data formatting | bytes 458752
  (9 shorter events, 0.1 us)
Async XLA Ops:
  8.3 4.3 %copy-start = (bf16[768,1792]{1,0:T(8,128)(2,1)S(1)}, bf16[768,1792]{1,0:T(8,128)(2,1)}, u32[]{:S(2)}) copy-start(bf16[768,1792]{1,0:T(8,128)(2,1)} %x_ref.1) | copy-start | bytes 8257540
  8.3 4.3 %copy-start.1 = (bf16[1792,576]{0,1:T(8,128)(2,1)S(1)}, bf16[1792,576]{0,1:T(8,128)(2,1)}, u32[]{:S(2)}) copy-start(bf16[1792,576]{0,1:T(8,128)(2,1)} %param.18) | copy-start | bytes 6193156
  8.3 4.3 %copy-start.2 = (bf16[64,1792]{1,0:T(8,128)(2,1)S(1)}, bf16[64,1792]{1,0:T(8,128)(2,1)}, u32[]{:S(2)}) copy-start(bf16[64,1792]{1,0:T(8,128)(2,1)} %n_ref.1) | copy-start | bytes 688132
  8.3 4.3 %copy-start.3 = (f32[512]{0:T(512)S(1)}, f32[512]{0:T(512)}, u32[]{:S(2)}) copy-start(f32[512]{0:T(512)} %param.17) | copy-start | bytes 6148
  73.0 11.7 %copy-start.4 = (bf16[32,512,128]{2,1,0:T(8,128)(2,1)S(1)}, bf16[32,512,128]{2,1,0:T(8,128)(2,1)}, u32[]{:S(2)}) copy-start(bf16[32,512,128]{2,1,0:T(8,128)(2,1)} %param.20) | copy-start | bytes 12582916

commit v4 on v3

--- a/solution.py
+++ b/solution.py
@@ -507,13 +507,7 @@
         across(s, p, True).start()
     gathered[s] = ho_ref[...]
     for p in range(PIECES):
-        for j in range(1, others + 1):
-            source = lax.rem(s - 2 * j + seq, seq)
-            over(j, source, p).wait_recv()
-            across(source, p, False).start()
-    for p in range(PIECES):
-        for j in range(others + 1):
-            across(lax.rem(sibling + 2 * j, seq), p, False).wait_recv()
+        across(sibling, p, False).wait_recv()
 
     def cut(q):
         return pl.ds(spans[q][0], spans[q][1])
@@ -541,45 +535,69 @@
             device_id_type=MESH,
         )
 
-    for q, (low, size) in enumerate(spans):
-        for n in range(low // tile, (low + size) // tile):
-            fetch(n).wait()
-            rows = gathered[...].reshape(seq * tokens, depth)
-            total[:, n * tile : (n + 1) * tile] = jnp.dot(
-                rows, w_ref[:, n * tile : (n + 1) * tile], preferred_element_type=jnp.float32
-            )
-
-        @pl.when(h == 0)
-        def _():
-            for c in range(heads - 1, 0, -1):
-                out_buf[c, :, cut(q)] = partial(c, q).astype(jnp.bfloat16)
-                send_right(c, q).start()
-
-        @pl.when(h == heads - 1)
-        def _():
-            for c in range(heads - 1):
-                out_buf[c, :, cut(q)] = partial(c, q).astype(jnp.bfloat16)
-                send_left(c, q).start()
-
-    for q in range(len(spans)):
-        for i in range(heads - 1):
-            right, left = heads - 1 - i, i
-
-            @pl.when((h > 0) & (h < right))
-            def _():
-                send_right(right, q).wait_recv()
-                out_buf[right, :, cut(q)] = (
-                    partial(right, q) + from_left[right, :, cut(q)].astype(jnp.float32)
-                ).astype(jnp.bfloat16)
-                send_right(right, q).start()
-
-            @pl.when((h > left) & (h < heads - 1))
-            def _():
-                send_left(left, q).wait_recv()
-                out_buf[left, :, cut(q)] = (
-                    partial(left, q) + from_right[left, :, cut(q)].astype(jnp.float32)
-                ).astype(jnp.bfloat16)
-                send_left(left, q).start()
+    per_chip = 2 * tokens // share
+
+    def chip_of(j):
+        return lax.rem(lax.div(s, 2) + j, seq // 2)
+
+    def multiply(j):
+        chip = chip_of(j)
+        rows = gathered[pl.ds(2 * chip, 2)].reshape(2 * tokens, depth)
+        place = pl.ds(pl.multiple_of(chip * 2 * tokens, 16), 2 * tokens)
+        for q, (low, size) in enumerate(spans):
+            for n in range(low // tile, (low + size) // tile):
+                if j == 0:
+                    fetch(n).wait()
+                total[place, n * tile : (n + 1) * tile] = jnp.dot(
+                    rows, w_ref[:, n * tile : (n + 1) * tile], preferred_element_type=jnp.float32
+                )
+            for k in range(per_chip):
+                c = chip * per_chip + k
+
+                @pl.when((h == 0) & (c > 0))
+                def _():
+                    out_buf[c, :, cut(q)] = partial(c, q).astype(jnp.bfloat16)
+                    send_right(c, q).start()
+
+                @pl.when((h == heads - 1) & (c < heads - 1))
+                def _():
+                    out_buf[c, :, cut(q)] = partial(c, q).astype(jnp.bfloat16)
+                    send_left(c, q).start()
+
+    def reduce(j):
+        for q in range(len(spans)):
+            for k in range(per_chip):
+                c = chip_of(j) * per_chip + k
+
+                @pl.when((h > 0) & (h < c))
+                def _():
+                    send_right(c, q).wait_recv()
+                    out_buf[c, :, cut(q)] = (
+                        partial(c, q) + from_left[c, :, cut(q)].astype(jnp.float32)
+                    ).astype(jnp.bfloat16)
+                    send_right(c, q).start()
+
+                @pl.when((h > c) & (h < heads - 1))
+                def _():
+                    send_left(c, q).wait_recv()
+                    out_buf[c, :, cut(q)] = (
+                        partial(c, q) + from_right[c, :, cut(q)].astype(jnp.float32)
+                    ).astype(jnp.bfloat16)
+                    send_left(c, q).start()
+
+    multiply(0)
+    for j in range(1, others + 1):
+        for p in range(PIECES):
+            source = lax.rem(s - 2 * j + seq, seq)
+            over(j, source, p).wait_recv()
+            across(source, p, False).start()
+    reduce(0)
+    for j in range(1, others + 1):
+        for p in range(PIECES):
+            across(lax.rem(sibling + 2 * j, seq), p, False).wait_recv()
+    for j in range(1, others + 1):
+        multiply(j)
+        reduce(j)
 
     for q in range(len(spans)):
 

time: 140 us -> 132 us (0.943)
  the two profiles are of different devices: /device:TPU:0 before, /device:TPU:2 now
where the time goes in v4:
time: 132 us; the launch traced here: 131 us
  Pallas kernels  114 us (86%)
  local copies, waits for them, and re-layouts  6.92 us (5%)
  matrix products  5.6 us (4%)
  other arithmetic  5.05 us (4%)
    pallas_call x1, Pallas kernels, latent_rows(): pl.pallas_call(functools.partial(latent_kernel, heads, seq), out_shape=(j...  57.9 us
    pallas_call x1, Pallas kernels, project(): pl.pallas_call(functools.partial(project_kernel, heads, seq, tile, spans)...  44 us
    pallas_call x1, Pallas kernels, attend(): pl.pallas_call(attend_kernel, out_shape=jax.ShapeDtypeStruct(ql.shape, jn...  11.7 us
    dot_general x1, matrix products, per_device(): jnp.einsum('thn,hnc->thc', queries[:, :, :NOPE], absorb_k, preferred_elem...  3.08 us

profile of v4, /device:TPU:2, one launch (start us, length us, event | category | flops | bytes accessed | tf_op | source)
XLA Modules:
  0.0 131.3 jit_solution(10024987788680988636)
XLA Ops:
  0.0 0.9 convert_reduce_fusion
  1.0 0.8 select_reduce_fusion
  1.8 0.1 select_reduce_fusion.1
  1.9 0.8 reshape.103
  2.7 1.0 select_reduce_fusion.3
  3.6 0.1 broadcast_in_dim.97
  3.7 0.1 reduce_sum.58
  3.8 0.8 select_reduce_fusion.2
  4.6 0.1 dynamic_slice.11
  4.7 0.1 add_convert_fusion
  4.8 0.8 fusion.10.bias_ref
  5.6 0.4 fusion.9
  6.0 0.1 pad_maximum_fusion
  6.1 1.1 slice.7
  7.2 1.1 slice.6
  8.3 0.0 copy-start
  8.3 0.0 copy-start.1
  8.3 0.0 copy-start.2
  8.3 0.0 copy-start.3
  8.4 3.1 %convert_bitcast_fusion = bf16[64,32,512]{2,0,1:T(8,128)(2,1)S(1)} fusion(bf16[32,128,512]{2,1,0:T(8,128)(2,1)} %param.19, bf16[64,32,128]{2,1,0:T(8,128)(2,1)S(1)} %slice.6), kind=kOutput, calls=%fused_computation.2 | convolution fusion | flops 269484032 | bytes 6815744 | tf_op jit(solution)/shard_map/thn,hnc->thc/dot_general | solution.py:752
  11.4 1.2 copy.21
  12.6 0.0 copy-done
  12.6 0.0 copy-done.1
  12.6 0.0 copy-done.2
  12.6 0.0 copy-done.3
  12.7 57.9 %shard_map.109 = (bf16[4,768,576]{2,1,0:T(8,128)(2,1)}, bf16[64,576]{1,0:T(8,128)(2,1)S(1)}) custom-call(bf16[768,1792]{1,0:T(8,128)(2,1)S(1)} %copy-done, bf16[64,1792]{1,0:T(8,128)(2,1)S(1)} %copy-done.2, bf16[576,1792]{1,0:T(8,128)(2,1)S(1)} %bitcast.22, f32[1,512]{1,0:T(1,128)S(1)} %bitcast.23, f32[208,64]{1,0:T(8,128)S(1)} %get-tuple-element.18.cos_ref, ...), custom_call_target="tpu_custom_call" | custom-call | tf_op jit(solution)/shard_map/pallas_call | solution.py:319
  70.5 0.0 copy-start.4
  70.5 11.7 %shard_map.110 = bf16[2048,512]{1,0:T(8,128)(2,1)S(1)} custom-call(s32[64]{0:T(128)S(1)} %get-tuple-element.14.start_ref, s32[64]{0:T(128)S(1)} %get-tuple-element.13.low_ref, s32[64]{0:T(128)S(1)} %get-tuple-element.11.len_ref, bf16[2048,512]{1,0:T(8,128)(2,1)S(1)} %bitcast.19, bf16[2048,64]{1,0:T(8,128)(2,1)S(1)} %bitcast.21, ...), custom_call_target="tpu_custom_call" | custom-call | tf_op jit(solution)/shard_map/pallas_call | solution.py:408
  82.2 0.0 copy-done.4
  82.2 2.5 %fusion.5 = bf16[32,8,8,128]{3,2,1,0:T(8,128)(2,1)S(1)} fusion(bf16[32,512,128]{2,1,0:T(8,128)(2,1)S(1)} %copy-done.4, bf16[64,32,512]{2,1,0:T(8,128)(2,1)S(1)} %bitcast.20), kind=kOutput, calls=%fused_computation.4 | convolution fusion | flops 268697600 | bytes 6815744 | tf_op jit(solution)/shard_map/thc,hcv->thv/dot_general | solution.py:770
  84.8 0.9 copy.36
  85.6 44.0 %shard_map.111 = bf16[64,1792]{1,0:T(8,128)(2,1)} custom-call(bf16[64,4096]{1,0:T(8,128)(2,1)} %bitcast.25, bf16[4096,1792]{1,0:T(8,128)(2,1)} %w_hbm.1), custom_call_target="tpu_custom_call" | custom-call | tf_op jit(solution)/shard_map/pallas_call | solution.py:654
  129.7 1.6 %copy.38 = bf16[64,1792]{1,0:T(8,128)(2,1)} copy(bf16[64,1792]{1,0:T(8,128)(2,1)} %shard_map.111) | data formatting | bytes 458752
  (9 shorter events, 0.1 us)
Async XLA Ops:
  8.3 4.3 %copy-start = (bf16[768,1792]{1,0:T(8,128)(2,1)S(1)}, bf16[768,1792]{1,0:T(8,128)(2,1)}, u32[]{:S(2)}) copy-start(bf16[768,1792]{1,0:T(8,128)(2,1)} %x_ref.1) | copy-start | bytes 8257540
  8.3 4.3 %copy-start.1 = (bf16[1792,576]{0,1:T(8,128)(2,1)S(1)}, bf16[1792,576]{0,1:T(8,128)(2,1)}, u32[]{:S(2)}) copy-start(bf16[1792,576]{0,1:T(8,128)(2,1)} %param.18) | copy-start | bytes 6193156
  8.3 4.3 %copy-start.2 = (bf16[64,1792]{1,0:T(8,128)(2,1)S(1)}, bf16[64,1792]{1,0:T(8,128)(2,1)}, u32[]{:S(2)}) copy-start(bf16[64,1792]{1,0:T(8,128)(2,1)} %n_ref.1) | copy-start | bytes 688132
  8.3 4.3 %copy-start.3 = (f32[512]{0:T(512)S(1)}, f32[512]{0:T(512)}, u32[]{:S(2)}) copy-start(f32[512]{0:T(512)} %param.17) | copy-start | bytes 6148
  70.5 11.7 %copy-start.4 = (bf16[32,512,128]{2,1,0:T(8,128)(2,1)S(1)}, bf16[32,512,128]{2,1,0:T(8,128)(2,1)}, u32[]{:S(2)}) copy-start(bf16[32,512,128]{2,1,0:T(8,128)(2,1)} %param.20) | copy-start | bytes 12582916
